TPU v7x, 32 devices: a whole 2x2x4 slice. The times are simulated.
32 devices in a mesh: group: 4 (over y, x), replica: 8 (over z, core).
Axes of the slice: x: 2, y: 2, z: 4, core: 2. Of those that a mesh axis runs over, the one named last changes fastest.
Arguments:
- tokens: bfloat16 [32, 1088, 1024], P('replica', 'group'), may hold values from -6 to 6
- segments: int32 [32, 1088], P('replica', 'group'), may hold values from 0 to 4, as said below
- routes: int32 [32, 1088, 8], P('replica', 'group'), may hold values from 0 to 31, all different within a row; in each aligned block of 272 rows (0 to 271, 272 to 543, ..., all dimensions but the last counted through in order) at most 96 rows name the same one
- norm_in: bfloat16 [1024], P('group'), may hold values from 0.25 to 1.75
- q_weight: bfloat16 [1024, 1024], P('group'), may hold values from -0.1875 to 0.1875
- key_weight: bfloat16 [1024, 512], P('group'), may hold values from -0.1875 to 0.1875
- value_weight: bfloat16 [1024, 512], P('group'), may hold values from -0.1875 to 0.1875
- q_gain: bfloat16 [64], P('group'), may hold values from 0.25 to 1.75
- k_gain: bfloat16 [64], P('group'), may hold values from 0.25 to 1.75
- o_weight: bfloat16 [1024, 1024], P('group'), may hold values from -1.5 to 1.5
- norm_post: bfloat16 [1024], P('group'), may hold values from 0.25 to 1.75
- router: bfloat16 [1024, 32], P('group'), may hold values from -0.09375 to 0.09375
- expert_in: bfloat16 [32, 1024, 1024], P('group'), may hold values from -0.1875 to 0.1875
- expert_out: bfloat16 [32, 512, 1024], P('group'), may hold values from -0.75 to 0.75
- cotangent: bfloat16 [32, 1088, 1024], P('replica', 'group'), may hold values from -6 to 6
Outputs:
- layer_out: bfloat16 [32, 1088, 1024], P('replica', 'group')
- tokens_grad: float32 [32, 1088, 1024], P('replica', 'group')
- norm_in_grad: float32 [1024], P('group')
- q_weight_grad: float32 [1024, 1024], P('group')
- k_weight_grad: float32 [1024, 512], P('group')
- v_weight_grad: float32 [1024, 512], P('group')
- q_gain_grad: float32 [64], P('group')
- k_gain_grad: float32 [64], P('group')
- o_weight_grad: float32 [1024, 1024], P('group')
- norm_post_grad: float32 [1024], P('group')
- router_grad: float32 [1024, 32], P('group')
- expert_in_grad: float32 [32, 1024, 1024], P('group')
- expert_out_grad: float32 [32, 512, 1024], P('group')
Inputs may be any that keep to these rules, and one draw needn't show every extreme that they name: `routes`: each token names 8 different experts. In each piece of 272 consecutive positions of a sequence, starting at a multiple of 272, no expert is named by more than 96 tokens, and some piece has an expert named by exactly 96. `segments`: segment numbers never fall along a sequence; the first position of every sequence holds 0 and the last holds 4.
All inputs are finite; a program needn't handle non-finite values.
Results may differ from a plain program's by a relative error of at most 0.022.
Values may be sent and summed in bfloat16 or wider, within the bound.
No kernel may reach another device: no remote copies, remote signals or barrier semaphores. Data moves between devices by JAX's collectives and lax.ppermute only.
A program may use at most 448 MiB of HBM per device.

v0:
```python
import math

import jax
import jax.numpy as jnp
from jax import lax
from jax.sharding import PartitionSpec as P

QUERY_HEADS = 16
KEY_VALUE_HEADS = 8
HEAD_SIZE = 64
E = 32
TOPK = 8


EPSILON = 1e-06
ROPE_BASE = 10000.0


def rms_scale(values):
    return lax.rsqrt(jnp.mean(values * values, axis=-1, keepdims=True) + EPSILON)


def angles(positions, head_dim):
    half_dim = head_dim // 2
    frequency = jnp.exp(
        -(2.0 * jnp.arange(half_dim, dtype=jnp.float32) / head_dim) * math.log(ROPE_BASE)
    )
    phase_table = positions.astype(jnp.float32)[..., None] * frequency
    phase_table = jnp.concatenate([phase_table, phase_table], axis=-1)
    return (jnp.cos(phase_table), jnp.sin(phase_table))


def rotate(values, cosine_table, sine_table):
    half_dim = values.shape[-1] // 2
    turned = jnp.concatenate([-values[..., half_dim:], values[..., :half_dim]], axis=-1)
    return values * cosine_table + turned * sine_table


def rotate_back(incoming, cosine_table, sine_table):
    half_dim = incoming.shape[-1] // 2
    moved_part = incoming * sine_table
    return incoming * cosine_table + jnp.concatenate(
        [moved_part[..., half_dim:], -moved_part[..., :half_dim]], axis=-1
    )


def norm_back(values, row_scale, gain_vec, incoming):
    weighted = incoming * gain_vec
    inner_mean = jnp.mean(weighted * values, axis=-1, keepdims=True)
    cubed = row_scale * row_scale * row_scale
    return (row_scale * weighted - values * cubed * inner_mean, incoming * values * row_scale)


def hidden_of(gate_up):
    half_width = gate_up.shape[-1] // 2
    return (jax.nn.silu(gate_up[..., :half_width]) * gate_up[..., half_width:]).astype(jnp.bfloat16)


def gate_grads(gate_up, grad_hidden):
    half_width = gate_up.shape[-1] // 2
    gate_part = gate_up[..., :half_width]
    up_part = gate_up[..., half_width:]
    sigma_gate = jax.nn.sigmoid(gate_part)
    grad_gate = grad_hidden * up_part * (sigma_gate * (1.0 + gate_part * (1.0 - sigma_gate)))
    grad_up = grad_hidden * gate_part * sigma_gate
    return jnp.concatenate([grad_gate, grad_up], axis=-1).astype(jnp.bfloat16)


def per_device(
    tokens,
    segments,
    routes,
    norm_in,
    q_weight,
    key_weight,
    value_weight,
    q_gain,
    k_gain,
    o_weight,
    norm_post,
    router,
    expert_in,
    expert_out,
    cotangent,
):
    group_size = lax.axis_size("group")
    sequence_total, partition_length, model_width = tokens.shape
    complete_length = partition_length * group_size
    capacity = (partition_length * TOPK * 4 // (3 * E) + 7) // 8 * 8
    query_grouping = QUERY_HEADS // KEY_VALUE_HEADS
    score_scale = 1.0 / math.sqrt(HEAD_SIZE)
    (
        gain_in,
        wq_full,
        wk_full,
        wv_full,
        gain_q,
        gain_k,
        output_weight_complete,
        gain_post,
        router_complete,
        seg_all,
    ) = (
        lax.all_gather(norm_in, "group", axis=0, tiled=True),
        lax.all_gather(q_weight, "group", axis=0, tiled=True),
        lax.all_gather(key_weight, "group", axis=0, tiled=True),
        lax.all_gather(value_weight, "group", axis=0, tiled=True),
        lax.all_gather(q_gain, "group", axis=0, tiled=True),
        lax.all_gather(k_gain, "group", axis=0, tiled=True),
        lax.all_gather(o_weight, "group", axis=0, tiled=True),
        lax.all_gather(norm_post, "group", axis=0, tiled=True),
        lax.all_gather(router, "group", axis=0, tiled=True),
        lax.all_gather(segments, "group", axis=1, tiled=True),
    )
    gain_in = gain_in.astype(jnp.float32)
    gain_q = gain_q.astype(jnp.float32)
    gain_k = gain_k.astype(jnp.float32)
    gain_post = gain_post.astype(jnp.float32)
    own_index = lax.axis_index("group") * partition_length + jnp.arange(
        partition_length, dtype=jnp.int32
    )
    starts = jnp.sum((seg_all[:, None, :] < segments[:, :, None]).astype(jnp.int32), axis=2)
    positions = own_index[None, :] - starts
    cosine_table, sine_table = angles(positions, HEAD_SIZE)
    cosine_per_head = cosine_table[:, :, None, :]
    sine_per_head = sine_table[:, :, None, :]
    allowed = (seg_all[:, None, :] == segments[:, :, None]) & (
        jnp.arange(complete_length, dtype=jnp.int32)[None, None, :] <= own_index[None, :, None]
    )
    inputs = tokens.astype(jnp.float32)
    scale_in = rms_scale(inputs)
    normed_low = (inputs * scale_in * gain_in).astype(jnp.bfloat16)
    query_pre = jnp.dot(normed_low, wq_full, preferred_element_type=jnp.float32).reshape(
        sequence_total, partition_length, QUERY_HEADS, HEAD_SIZE
    )
    key_pre = jnp.dot(normed_low, wk_full, preferred_element_type=jnp.float32).reshape(
        sequence_total, partition_length, KEY_VALUE_HEADS, HEAD_SIZE
    )
    value_low = jnp.dot(normed_low, wv_full, preferred_element_type=jnp.float32).astype(
        jnp.bfloat16
    )
    query_scale = rms_scale(query_pre)
    query_lowered = rotate(query_pre * query_scale * gain_q, cosine_per_head, sine_per_head).astype(
        jnp.bfloat16
    )
    key_scale = rms_scale(key_pre)
    key_lowered = rotate(key_pre * key_scale * gain_k, cosine_per_head, sine_per_head).astype(
        jnp.bfloat16
    )
    key_lowered = key_lowered.reshape(sequence_total, partition_length, KEY_VALUE_HEADS * HEAD_SIZE)
    key_gathered, value_gathered = (
        lax.all_gather(key_lowered, "group", axis=1, tiled=True),
        lax.all_gather(value_low, "group", axis=1, tiled=True),
    )
    query_heads_split = query_lowered.reshape(
        sequence_total, partition_length, KEY_VALUE_HEADS, query_grouping, HEAD_SIZE
    ).transpose(2, 0, 3, 1, 4)
    key_heads_split = key_gathered.reshape(
        sequence_total, complete_length, KEY_VALUE_HEADS, HEAD_SIZE
    ).transpose(2, 0, 1, 3)
    value_heads_split = value_gathered.reshape(
        sequence_total, complete_length, KEY_VALUE_HEADS, HEAD_SIZE
    ).transpose(2, 0, 1, 3)

    def masked_scores(q_head, k_head):
        scores = (
            jnp.einsum("sgqd,skd->sgqk", q_head, k_head, preferred_element_type=jnp.float32)
            * score_scale
        )
        return jnp.where(allowed[:, None], scores, -1e30)

    def attend(packed):
        q_head, k_head, v_head = packed
        scores = masked_scores(q_head, k_head)
        row_max = jnp.max(scores, axis=-1, keepdims=True)
        raised = jnp.exp(scores - row_max)
        row_sum = jnp.sum(raised, axis=-1, keepdims=True)
        soft_weights = (raised / row_sum).astype(jnp.bfloat16)
        out_head = jnp.einsum(
            "sgqk,skd->sgqd", soft_weights, v_head, preferred_element_type=jnp.float32
        )
        return (out_head.astype(jnp.bfloat16), (row_max + jnp.log(row_sum))[..., 0])

    attended, log_norm = lax.map(attend, (query_heads_split, key_heads_split, value_heads_split))
    attention_lowered = attended.transpose(1, 3, 0, 2, 4).reshape(
        sequence_total, partition_length, QUERY_HEADS * HEAD_SIZE
    )
    attn_out = jnp.dot(
        attention_lowered, output_weight_complete, preferred_element_type=jnp.float32
    )
    middle = inputs + attn_out
    scale_post = rms_scale(middle)
    post_lowered = (middle * scale_post * gain_post).astype(jnp.bfloat16)
    logits = jnp.dot(post_lowered, router_complete, preferred_element_type=jnp.float32)
    picked = jnp.take_along_axis(logits, routes, axis=2)
    picked_max = jnp.max(picked, axis=2, keepdims=True)
    gate_exp = jnp.exp(picked - picked_max)
    gate_vals = gate_exp / jnp.sum(gate_exp, axis=2, keepdims=True)
    flat_routes = routes.reshape(sequence_total, partition_length * TOPK)
    hit_table = (flat_routes[:, :, None] == jnp.arange(E, dtype=jnp.int32)[None, None, :]).astype(
        jnp.int32
    )
    slot_rank = jnp.sum(jnp.cumsum(hit_table, axis=1) * hit_table, axis=2) - 1
    slot_index = flat_routes * capacity + slot_rank
    slot_table = (
        jnp.zeros((sequence_total, E * capacity), jnp.int32)
        .at[jnp.arange(sequence_total, dtype=jnp.int32)[:, None], slot_index]
        .set(jnp.arange(partition_length * TOPK, dtype=jnp.int32)[None, :] + 1)
    )
    filled = slot_table > 0
    assignment = jnp.maximum(slot_table - 1, 0)
    source_row = assignment // TOPK
    slot_rows = jnp.take_along_axis(post_lowered, source_row[:, :, None], axis=1)
    slot_rows = jnp.where(filled[:, :, None], slot_rows, jnp.zeros((), jnp.bfloat16)).reshape(
        sequence_total, E, capacity, model_width
    )
    received = lax.all_to_all(slot_rows, "group", split_axis=1, concat_axis=0, tiled=True)
    gate_up = jnp.einsum("becd,edf->becf", received, expert_in, preferred_element_type=jnp.float32)
    hidden_low = hidden_of(gate_up)
    outputs = jnp.einsum(
        "becf,efd->becd", hidden_low, expert_out, preferred_element_type=jnp.float32
    ).astype(jnp.bfloat16)
    slot_out = lax.all_to_all(outputs, "group", split_axis=0, concat_axis=1, tiled=True)
    flat_out = slot_out.reshape(sequence_total, E * capacity, model_width)
    chosen = jnp.take_along_axis(flat_out, slot_index[:, :, None], axis=1).reshape(
        sequence_total, partition_length, TOPK, model_width
    )
    final_sum = middle + jnp.sum(gate_vals[..., None] * chosen.astype(jnp.float32), axis=2)
    layer_out = final_sum.astype(jnp.bfloat16)
    grad_final = cotangent.astype(jnp.float32)
    grad_gates = jnp.sum(chosen.astype(jnp.float32) * grad_final[:, :, None, :], axis=3)
    slot_grad = (
        (gate_vals[..., None] * grad_final[:, :, None, :])
        .astype(jnp.bfloat16)
        .reshape(sequence_total, partition_length * TOPK, model_width)
    )
    slot_grads = jnp.take_along_axis(slot_grad, assignment[:, :, None], axis=1)
    slot_grads = jnp.where(filled[:, :, None], slot_grads, jnp.zeros((), jnp.bfloat16)).reshape(
        sequence_total, E, capacity, model_width
    )
    received_grads = lax.all_to_all(slot_grads, "group", split_axis=1, concat_axis=0, tiled=True)
    grad_hidden = jnp.einsum(
        "becd,efd->becf", received_grads, expert_out, preferred_element_type=jnp.float32
    )
    grad_gate_up = gate_grads(gate_up, grad_hidden)
    expert_out_grad = jnp.einsum(
        "becf,becd->efd", hidden_of(gate_up), received_grads, preferred_element_type=jnp.float32
    )
    expert_in_grad = jnp.einsum(
        "becd,becf->edf", received, grad_gate_up, preferred_element_type=jnp.float32
    )
    row_grads = jnp.einsum(
        "becf,edf->becd", grad_gate_up, expert_in, preferred_element_type=jnp.float32
    ).astype(jnp.bfloat16)
    slot_back = lax.all_to_all(row_grads, "group", split_axis=0, concat_axis=1, tiled=True)
    back_rows = jnp.take_along_axis(
        slot_back.reshape(sequence_total, E * capacity, model_width), slot_index[:, :, None], axis=1
    )
    grad_post = jnp.sum(
        back_rows.reshape(sequence_total, partition_length, TOPK, model_width).astype(jnp.float32),
        axis=2,
    )
    gate_mean = jnp.sum(gate_vals * grad_gates, axis=2, keepdims=True)
    grad_picked = gate_vals * (grad_gates - gate_mean)
    expert_match = routes[..., None] == jnp.arange(E, dtype=jnp.int32)[None, None, None, :]
    logit_gradient = jnp.sum(jnp.where(expert_match, grad_picked[..., None], 0.0), axis=2).astype(
        jnp.bfloat16
    )
    router_grad = jnp.einsum(
        "ijy,ijk->yk", post_lowered, logit_gradient, preferred_element_type=jnp.float32
    )
    grad_post = grad_post + jnp.einsum(
        "zpn,in->zpi", logit_gradient, router_complete, preferred_element_type=jnp.float32
    )
    grad_mid_norm, post_terms = norm_back(middle, scale_post, gain_post, grad_post)
    grad_middle = grad_final + grad_mid_norm
    norm_post_grad = jnp.sum(post_terms, axis=(0, 1))
    attention_lowered_gradient = grad_middle.astype(jnp.bfloat16)
    o_weight_grad = jnp.einsum(
        "tow,tor->wr",
        attention_lowered,
        attention_lowered_gradient,
        preferred_element_type=jnp.float32,
    )
    attended_gradient = jnp.einsum(
        "gui,pi->gup",
        attention_lowered_gradient,
        output_weight_complete,
        preferred_element_type=jnp.float32,
    ).astype(jnp.bfloat16)
    head_gradient = attended_gradient.reshape(
        sequence_total, partition_length, KEY_VALUE_HEADS, query_grouping, HEAD_SIZE
    ).transpose(2, 0, 3, 1, 4)

    def attend_back(packed):
        q_head, k_head, v_head, grad_head, norm_head = packed
        soft_f32 = jnp.exp(masked_scores(q_head, k_head) - norm_head[..., None])
        grad_soft = jnp.einsum(
            "sgqd,skd->sgqk", grad_head, v_head, preferred_element_type=jnp.float32
        )
        row_dot = jnp.sum(soft_f32 * grad_soft, axis=-1, keepdims=True)
        grad_scores = (soft_f32 * (grad_soft - row_dot)).astype(jnp.bfloat16)
        grad_q = (
            jnp.einsum("sgqk,skd->sgqd", grad_scores, k_head, preferred_element_type=jnp.float32)
            * score_scale
        )
        key_gradient = (
            jnp.einsum("sgqk,sgqd->skd", grad_scores, q_head, preferred_element_type=jnp.float32)
            * score_scale
        )
        value_gradient = jnp.einsum(
            "sgqk,sgqd->skd",
            soft_f32.astype(jnp.bfloat16),
            grad_head,
            preferred_element_type=jnp.float32,
        )
        return (grad_q, key_gradient, value_gradient)

    grad_q, key_gradient, value_gradient = lax.map(
        attend_back,
        (query_heads_split, key_heads_split, value_heads_split, head_gradient, log_norm),
    )
    grad_q = grad_q.transpose(1, 3, 0, 2, 4).reshape(
        sequence_total, partition_length, QUERY_HEADS, HEAD_SIZE
    )
    key_gradient_gathered = key_gradient.transpose(1, 2, 0, 3).reshape(
        sequence_total, complete_length, KEY_VALUE_HEADS * HEAD_SIZE
    )
    value_gradient_gathered = value_gradient.transpose(1, 2, 0, 3).reshape(
        sequence_total, complete_length, KEY_VALUE_HEADS * HEAD_SIZE
    )
    key_gradient_local, grad_value_own = (
        lax.psum_scatter(
            key_gradient_gathered.astype(jnp.bfloat16), "group", scatter_dimension=1, tiled=True
        ).astype(jnp.float32),
        lax.psum_scatter(
            value_gradient_gathered.astype(jnp.bfloat16), "group", scatter_dimension=1, tiled=True
        ).astype(jnp.float32),
    )
    grad_query_rot = rotate_back(grad_q, cosine_per_head, sine_per_head)
    grad_query_pre, query_terms = norm_back(query_pre, query_scale, gain_q, grad_query_rot)
    q_gain_grad = jnp.sum(query_terms, axis=(0, 1, 2))
    grad_key_rot = rotate_back(
        key_gradient_local.reshape(sequence_total, partition_length, KEY_VALUE_HEADS, HEAD_SIZE),
        cosine_per_head,
        sine_per_head,
    )
    key_gradient_unrotated, key_terms = norm_back(key_pre, key_scale, gain_k, grad_key_rot)
    k_gain_grad = jnp.sum(key_terms, axis=(0, 1, 2))
    grad_q_low = grad_query_pre.astype(jnp.bfloat16).reshape(
        sequence_total, partition_length, QUERY_HEADS * HEAD_SIZE
    )
    key_lowered_gradient = key_gradient_unrotated.astype(jnp.bfloat16).reshape(
        sequence_total, partition_length, KEY_VALUE_HEADS * HEAD_SIZE
    )
    grad_v_low = grad_value_own.astype(jnp.bfloat16)
    q_weight_grad = jnp.einsum(
        "slc,slh->ch", normed_low, grad_q_low, preferred_element_type=jnp.float32
    )
    k_weight_grad = jnp.einsum(
        "slc,slh->ch", normed_low, key_lowered_gradient, preferred_element_type=jnp.float32
    )
    v_weight_grad = jnp.einsum(
        "slc,slh->ch", normed_low, grad_v_low, preferred_element_type=jnp.float32
    )
    grad_normed = jnp.einsum("slh,ch->slc", grad_q_low, wq_full, preferred_element_type=jnp.float32)
    grad_normed = grad_normed + jnp.einsum(
        "slh,ch->slc", key_lowered_gradient, wk_full, preferred_element_type=jnp.float32
    )
    grad_normed = grad_normed + jnp.einsum(
        "slh,ch->slc", grad_v_low, wv_full, preferred_element_type=jnp.float32
    )
    grad_in_norm, input_terms = norm_back(inputs, scale_in, gain_in, grad_normed)
    tokens_grad = grad_middle + grad_in_norm
    norm_in_grad = jnp.sum(input_terms, axis=(0, 1))
    shard_in, shard_q, shard_k, shard_v, shard_qg, shard_kg, shard_o, shard_post, shard_router = (
        lax.psum_scatter(
            norm_in_grad.astype(jnp.bfloat16), "group", scatter_dimension=0, tiled=True
        ).astype(jnp.float32),
        lax.psum_scatter(
            q_weight_grad.astype(jnp.bfloat16), "group", scatter_dimension=0, tiled=True
        ).astype(jnp.float32),
        lax.psum_scatter(
            k_weight_grad.astype(jnp.bfloat16), "group", scatter_dimension=0, tiled=True
        ).astype(jnp.float32),
        lax.psum_scatter(
            v_weight_grad.astype(jnp.bfloat16), "group", scatter_dimension=0, tiled=True
        ).astype(jnp.float32),
        lax.psum_scatter(
            q_gain_grad.astype(jnp.bfloat16), "group", scatter_dimension=0, tiled=True
        ).astype(jnp.float32),
        lax.psum_scatter(
            k_gain_grad.astype(jnp.bfloat16), "group", scatter_dimension=0, tiled=True
        ).astype(jnp.float32),
        lax.psum_scatter(
            o_weight_grad.astype(jnp.bfloat16), "group", scatter_dimension=0, tiled=True
        ).astype(jnp.float32),
        lax.psum_scatter(
            norm_post_grad.astype(jnp.bfloat16), "group", scatter_dimension=0, tiled=True
        ).astype(jnp.float32),
        lax.psum_scatter(
            router_grad.astype(jnp.bfloat16), "group", scatter_dimension=0, tiled=True
        ).astype(jnp.float32),
    )
    (
        shard_in,
        shard_q,
        shard_k,
        shard_v,
        shard_qg,
        shard_kg,
        shard_o,
        shard_post,
        shard_router,
        expert_in_grad,
        expert_out_grad,
    ) = (
        lax.psum(shard_in.astype(jnp.bfloat16), "replica").astype(jnp.float32),
        lax.psum(shard_q.astype(jnp.bfloat16), "replica").astype(jnp.float32),
        lax.psum(shard_k.astype(jnp.bfloat16), "replica").astype(jnp.float32),
        lax.psum(shard_v.astype(jnp.bfloat16), "replica").astype(jnp.float32),
        lax.psum(shard_qg.astype(jnp.bfloat16), "replica").astype(jnp.float32),
        lax.psum(shard_kg.astype(jnp.bfloat16), "replica").astype(jnp.float32),
        lax.psum(shard_o.astype(jnp.bfloat16), "replica").astype(jnp.float32),
        lax.psum(shard_post.astype(jnp.bfloat16), "replica").astype(jnp.float32),
        lax.psum(shard_router.astype(jnp.bfloat16), "replica").astype(jnp.float32),
        lax.psum(expert_in_grad.astype(jnp.bfloat16), "replica").astype(jnp.float32),
        lax.psum(expert_out_grad.astype(jnp.bfloat16), "replica").astype(jnp.float32),
    )
    return (
        layer_out,
        tokens_grad,
        shard_in,
        shard_q,
        shard_k,
        shard_v,
        shard_qg,
        shard_kg,
        shard_o,
        shard_post,
        shard_router,
        expert_in_grad,
        expert_out_grad,
    )


def solution(mesh):
    placed = (
        P("replica", "group", None),
        P("replica", "group"),
        P("replica", "group", None),
        P("group"),
        P("group", None),
        P("group", None),
        P("group", None),
        P("group"),
        P("group"),
        P("group", None),
        P("group"),
        P("group", None),
        P("group", None, None),
        P("group", None, None),
        P("replica", "group", None),
    )
    return jax.shard_map(
        per_device,
        mesh=mesh,
        in_specs=placed,
        out_specs=(
            P("replica", "group", None),
            P("replica", "group", None),
            P("group"),
            P("group", None),
            P("group", None),
            P("group", None),
            P("group"),
            P("group"),
            P("group", None),
            P("group"),
            P("group", None),
            P("group", None, None),
            P("group", None, None),
        ),
        check_vma=False,
    )
```

profile of v0, /device:TPU:0, one launch (start us, length us, event | category | flops | bytes accessed | tf_op | source)
XLA Modules:
  0.0 4015.9 jit_solution(1506566828891311131)
XLA Ops:
  84.1 63.6 %reduce-window.6 = s32[4,32,17,128]{3,2,1,0:T(8,128)S(1)} reduce-window(s32[4,32,17,128]{3,2,1,0:T(8,128)} %fusion.99, s32[]{:T(128)} %copy.454), window={size=1x1x1x128 pad=0_0x0_0x0_0x127_0}, to_apply=%region_11.12 | reduce-window | flops 35373056 | bytes 2228228 | tf_op jit(solution)/shard_map/reduce-window
  156.6 32.3 scatter_custom_fusion
  247.2 104.5 %while.28 = (s32[]{:T(128)}, bf16[8,4,2,272,64]{3,4,2,1,0:T(8,128)(2,1)}, f32[8,4,2,272]{3,2,1,0:T(2,128)}, bf16[8,4,2,272,64]{3,4,2,1,0:T(8,128)(2,1)}, bf16[8,...) while((s32[]{:T(128)}, ...), condition=%wide.region_7.8_spmd.clone, body=%wide.region_4.7_spmd.clone.sunk | while | flops 636991360 | bytes 35504484 | solution.py:184
  364.6 178.0 %gather_fusion.1 = bf16[12288,1024]{1,0:T(8,128)(2,1)} fusion(bf16[4,272,1024]{2,1,0:T(8,128)(2,1)S(1)} %multiply_convert_fusion.2, s32[12288]{0:T(1024)S(1)} %bitcast.363), kind=kCustom, calls=%fused_computation.3 | custom fusion | bytes 50429952 | tf_op jit(solution)/shard_map/jit(take_along_axis)/gather | solution.py:213
  564.8 271.2 %all_to_all.66 = bf16[4,32,96,1024]{3,2,0,1:T(8,128)(2,1)S(1)} all-to-all(bf16[4,32,96,1024]{3,2,0,1:T(8,128)(2,1)} %fusion.64), channel_id=1, replica_groups=mesh['group'=4,'replica'=8] {'group'}, dimensions={1} | all-to-all | bytes 50331648 | tf_op jit(solution)/shard_map/all_to_all | solution.py:217
  844.5 39.7 convolution_bitcast_fusion.1
  906.2 22.3 convert_bitcast_fusion.2
  965.3 260.4 %all_gather.47 = bf16[1024,32]{0,1:T(8,128)(2,1)S(1)} all-gather(bf16[256,32]{0,1:T(8,128)(2,1)S(1)} %copy-done.84), channel_id=1, replica_groups=mesh['group'=4,'replica'=8] {'group'}, dimensions={0}, use_global_device_ids=true | all-gather | bytes 81920 | tf_op jit(solution)/shard_map/all_gather | solution.py:112
  1227.2 82.3 %gather_fusion = f32[8704]{0:T(1024)S(1)} fusion(f32[4,272,32]{1,2,0:T(8,128)S(1)} %fusion.117, s32[8704]{0:T(1024)S(1)} %reshape.473), kind=kCustom, calls=%fused_computation.2 | custom fusion | bytes 174080 | tf_op jit(solution)/shard_map/jit(take_along_axis)/gather | solution.py:195
  1331.8 171.3 %gather_fusion.3 = bf16[8704,1024]{1,0:T(8,128)(2,1)} fusion(bf16[4,3072,1024]{2,1,0:T(8,128)(2,1)} %bitcast.362, s32[8704]{0:T(1024)S(1)} %copy-done.5), kind=kCustom, calls=%fused_computation.clone | custom fusion | bytes 35721216 | tf_op jit(solution)/shard_map/jit(take_along_axis)/gather | solution.py:225
  1528.6 334.2 %gather_fusion.2 = bf16[12288,1024]{1,0:T(8,128)(2,1)} fusion(bf16[4,2176,1024]{2,1,0:T(8,128)(2,1)} %fusion.57, s32[12288]{0:T(1024)S(1)} %bitcast.364), kind=kCustom, calls=%fused_computation.4 | custom fusion | bytes 50429952 | tf_op jit(solution)/shard_map/jit(take_along_axis)/gather | solution.py:237
  1885.0 276.7 %all_to_all.67 = bf16[4,32,96,1024]{3,2,0,1:T(8,128)(2,1)S(1)} all-to-all(bf16[4,32,96,1024]{3,2,0,1:T(8,128)(2,1)} %fusion.63), channel_id=1, replica_groups=mesh['group'=4,'replica'=8] {'group'}, dimensions={1} | all-to-all | bytes 50331648 | tf_op jit(solution)/shard_map/all_to_all | solution.py:241
  2170.1 39.6 fusion.60
  2209.7 37.1 convert_bitcast_fusion.1
  2277.0 269.3 %all-to-all-done.3 = bf16[16,8,96,1024]{3,2,1,0:T(8,128)(2,1)} async-done(((bf16[16,8,96,1024]{3,2,1,0:T(8,128)(2,1)}), bf16[16,8,96,1024]{3,2,1,0:T(8,128)(2,1)}, u32[]{:S(2)}, u32[]{:S(2)}) %all-to-all-start.3) | async-done | bytes 25165856 | tf_op jit(solution)/shard_map/all_to_all | solution.py:255
  2568.0 171.5 %gather_fusion.4 = bf16[8704,1024]{1,0:T(8,128)(2,1)} fusion(bf16[4,3072,1024]{2,1,0:T(8,128)(2,1)} %bitcast.361, s32[8704]{0:T(1024)S(1)} %copy-done.6), kind=kCustom, calls=%fused_computation.1.clone | custom fusion | bytes 35721216 | tf_op jit(solution)/shard_map/jit(take_along_axis)/gather | solution.py:256
  2739.5 59.3 %convert_reduce_fusion = (f32[4,272,1024]{2,1,0:T(8,128)S(1)}, f32[4,272,1024]{2,1,0:T(8,128)S(1)}) fusion(bf16[4,2176,1024]{2,1,0:T(8,128)(2,1)} %bitcast.374, pred[4,2176]{1,0:T(4,128)(4,1)S(1)} %copy-done.68, bf16[4,2176,1024]{2,1,0:T(8,128)(2,1)} %bitcast.366, f32[4,272,8]{2,1,0:T(8,128)S(1)} %copy-done.28), kind=kLoop, calls=%fused_computation.74 | loop fusion | flops 60162048 | bytes 44608000 | tf_op jit(solution)/shard_map/reduce_sum | solution.py:259
  2816.8 284.4 %while.29 = (s32[]{:T(128)}, f32[8,4,2,272,64]{3,4,2,0,1:T(8,128)}, bf16[8,4,1088,64]{2,3,1,0:T(8,128)(2,1)}, bf16[8,4,1088,64]{2,3,1,0:T(8,128)(2,1)}, bf16[8,4...) while((s32[]{:T(128)}, f32[8,4,2,272,64]{3,4,2,0,1:T(8,128)}, ...), condition=%wide.region_23.25_spmd.clone, body=%wide.region_21.24_spmd.clone.sunk | while | flops 1539282816 | bytes 157120432 | solution.py:319
  3228.3 52.3 %reduce-scatter.7.cloned.1.call-done = bf16[4,272,512]{2,1,0:T(8,128)(2,1)} async-done(((bf16[4,1088,512]{2,1,0:T(8,128)(2,1)}), bf16[4,272,512]{2,1,0:T(8,128)(2,1)}) %reduce-scatter.7.cloned.1.call-update) | async-done | bytes 1114128 | tf_op jit(solution)/shard_map/reduce_scatter | solution.py:333
  3307.7 37.8 bitcast_convert_fusion
  3345.5 25.5 bitcast_convert_fusion.1
  3388.3 31.3 reduce-scatter.11.cloned.1.call-done
  3446.7 29.0 all-reduce.7
  3484.2 490.6 %all-reduce.16.cloned.1.call-done = (bf16[256,1024]{1,0:T(8,128)(2,1)}, bf16[256,512]{1,0:T(8,128)(2,1)}, bf16[256,512]{1,0:T(8,128)(2,1)}, bf16[256,1024]{1,0:T...) async-done(((bf16[256,1024]{1,0:T(8,128)(2,1)}, bf16[256,512]{1,0:T(8,128)(2,1)}, bf16[256,512]{1,0:T(8,128)(2,1)}, ...) | async-done | bytes 26738704 | tf_op jit(solution)/shard_map/psum | solution.py:419
  (569 shorter events, 1021.6 us)
Async XLA Ops:
  7.2 45.4 %all-gather.12.cloned.1.call-start = ((), (), s32[]{:S(2)}) async-start(), calls=%async_computation.11 | async-start | bytes 1310720 | tf_op jit(solution)/shard_map/all_gather | solution.py:106
  7.9 68.7 %all-gather.16.cloned.1.call-start = ((), (), s32[]{:S(2)}) async-start(), calls=%async_computation.13 | async-start | bytes 1310720 | tf_op jit(solution)/shard_map/all_gather | solution.py:107
  8.7 190.5 %all-gather.10.cloned.1.call-start = ((), (), s32[]{:S(2)}) async-start(), calls=%async_computation.10 | async-start | bytes 2621440 | tf_op jit(solution)/shard_map/all_gather | solution.py:105
  9.4 214.7 %all-gather.14.cloned.1.call-start = ((), (), s32[]{:S(2)}) async-start(), calls=%async_computation.12 | async-start | bytes 5570560 | tf_op jit(solution)/shard_map/all_gather | solution.py:152
  19.6 179.5 %copy-start.76 = (f32[4,1,256]{2,1,0:T(1,128)}, f32[4,1,256]{2,1,0:T(1,128)S(1)}, u32[]{:S(2)}) copy-start(f32[4,1,256]{2,1,0:T(1,128)S(1)} %convert_element_type.288) | copy-start | bytes 12292
  76.5 159.1 %all-gather.18.cloned.1.call-start = ((), (), s32[]{:S(2)}) async-start(), calls=%async_computation.14 | async-start | bytes 5570560 | tf_op jit(solution)/shard_map/all_gather | solution.py:153
  81.2 274.8 %all-gather.20.cloned.1.call-start = ((), (), s32[]{:S(2)}) async-start(), calls=%async_computation.15 | async-start | bytes 2621440 | tf_op jit(solution)/shard_map/all_gather | solution.py:110
  364.5 178.1 %copy-start = (bf16[4,272,1024]{2,1,0:T(8,128)(2,1)}, bf16[4,272,1024]{2,1,0:T(8,128)(2,1)S(1)}, u32[]{:S(2)}) copy-start(bf16[4,272,1024]{2,1,0:T(8,128)(2,1)S(1)} %multiply_convert_fusion.2) | copy-start | bytes 6684676
  364.6 178.1 %copy-start.63 = (pred[4,32,96]{2,0,1:T(4,128)(4,1)S(1)}, pred[4,32,96]{2,0,1:T(4,128)(4,1)}, u32[]{:S(2)}) copy-start(pred[4,32,96]{2,0,1:T(4,128)(4,1)} %copy.324) | copy-start | bytes 36868
  364.6 178.1 %copy-start.69 = (pred[4,32,96]{2,0,1:T(4,128)(4,1)S(1)}, pred[4,32,96]{2,0,1:T(4,128)(4,1)}, u32[]{:S(2)}) copy-start(pred[4,32,96]{2,0,1:T(4,128)(4,1)} %copy.325) | copy-start | bytes 36868
  949.7 360.8 %all-to-all-start.1 = ((bf16[16,8,96,1024]{3,2,1,0:T(8,128)(2,1)}), bf16[16,8,96,1024]{3,2,1,0:T(8,128)(2,1)}, u32[]{:S(2)}, u32[]{:S(2)}) async-start(bf16[16,8,96,1024]{3,2,1,0:T(8,128)(2,1)} %copy.329), calls=%async_computation.1 | async-start | bytes 50331648 | tf_op jit(solution)/shard_map/all_to_all | solution.py:223
  958.5 267.9 %copy-start.1 = (bf16[4,272,1024]{2,1,0:T(8,128)(2,1)S(1)}, bf16[4,272,1024]{2,1,0:T(8,128)(2,1)}, u32[]{:S(2)}) copy-start(bf16[4,272,1024]{2,1,0:T(8,128)(2,1)} %copy-done) | copy-start | bytes 6684676
  1528.5 334.3 %copy-start.64 = (pred[4,32,96]{2,0,1:T(4,128)(4,1)S(1)}, pred[4,32,96]{2,0,1:T(4,128)(4,1)}, u32[]{:S(2)}) copy-start(pred[4,32,96]{2,0,1:T(4,128)(4,1)} %copy.324) | copy-start | bytes 36868
  1528.5 334.3 %copy-start.70 = (pred[4,32,96]{2,0,1:T(4,128)(4,1)S(1)}, pred[4,32,96]{2,0,1:T(4,128)(4,1)}, u32[]{:S(2)}) copy-start(pred[4,32,96]{2,0,1:T(4,128)(4,1)} %copy.331) | copy-start | bytes 36868
  2268.1 278.3 %all-to-all-start.3 = ((bf16[16,8,96,1024]{3,2,1,0:T(8,128)(2,1)}), bf16[16,8,96,1024]{3,2,1,0:T(8,128)(2,1)}, u32[]{:S(2)}, u32[]{:S(2)}) async-start(bf16[16,8,96,1024]{3,2,1,0:T(8,128)(2,1)} %copy.336), calls=%async_computation.3 | async-start | bytes 50331648 | tf_op jit(solution)/shard_map/all_to_all | solution.py:255
  2276.6 946.0 %all-reduce.14.cloned.1.call-start = ((), (), s32[]{:S(2)}) async-start(), calls=%async_computation.22 | async-start | bytes 8912896
  2277.0 521.7 %copy-start.41 = (bf16[4,272,32]{1,2,0:T(8,128)(2,1)}, bf16[4,272,32]{1,2,0:T(8,128)(2,1)S(1)}, u32[]{:S(2)}) copy-start(bf16[4,272,32]{1,2,0:T(8,128)(2,1)S(1)} %select_reduce_fusion) | copy-start | bytes 208900
  3115.0 165.6 %reduce-scatter.7.cloned.1.call-start = ((), (), s32[]{:S(2)}) async-start(), calls=%async_computation.16 | async-start | bytes 5570560 | tf_op jit(solution)/shard_map/reduce_scatter | solution.py:333
  3126.8 244.3 %reduce-scatter.9.cloned.1.call-start = ((), (), s32[]{:S(2)}) async-start(), calls=%async_computation.17 | async-start | bytes 2621440 | tf_op jit(solution)/shard_map/reduce_scatter | solution.py:380
  3207.9 163.1 %reduce-scatter.15.cloned.1.call-start = ((), (), s32[]{:S(2)}) async-start(), calls=%async_computation.20 | async-start | bytes 2621440 | tf_op jit(solution)/shard_map/reduce_scatter | solution.py:395
  3215.7 172.7 %reduce-scatter.13.cloned.1.call-start = ((), (), s32[]{:S(2)}) async-start(), calls=%async_computation.19 | async-start | bytes 1310720 | tf_op jit(solution)/shard_map/reduce_scatter | solution.py:386
  3228.2 191.4 %reduce-scatter.11.cloned.1.call-start = ((), (), s32[]{:S(2)}) async-start(), calls=%async_computation.18 | async-start | bytes 1310720 | tf_op jit(solution)/shard_map/reduce_scatter | solution.py:383
  3306.4 140.2 %reduce-scatter.17.cloned.1.call-start = ((), (), s32[]{:S(2)}) async-start(), calls=%async_computation.21 | async-start | bytes 81920 | tf_op jit(solution)/shard_map/reduce_scatter | solution.py:401
  3307.6 667.2 %all-reduce.16.cloned.1.call-start = ((), (), s32[]{:S(2)}) async-start(), calls=%async_computation.23 | async-start | bytes 53477376 | tf_op jit(solution)/shard_map/psum | solution.py:419
  (103 other events, 2094.9 us)
Sparse Core Ops, SparseCore 0:
  9.9 29.6 all-gather.11
  41.3 26.6 all-gather.15
  69.9 35.3 all-gather.9
  107.5 54.9 all-gather.13
  164.2 54.8 all-gather.17
  220.8 35.3 all-gather.19
  3115.1 107.4 all-reduce.13
  3225.7 54.8 reduce-scatter.6
  3283.6 35.1 reduce-scatter.8
  3321.9 35.1 reduce-scatter.14
  3360.6 27.7 reduce-scatter.12
  3391.9 27.6 reduce-scatter.10
  3422.9 23.6 reduce-scatter.16
  3450.7 524.0 all-reduce.15
where the time goes:
time: 4050 us; the launch traced here: 4020 us
  local copies, waits for them, and re-layouts  1260 us (31%)
  blocking collectives  881 us (22%)
  waiting for transfers between devices  865 us (21%)
  matrix products  526 us (13%)
  other arithmetic  452 us (11%)
    psum x1, waiting for transfers between devices, per_device(): lax.psum(shard_q.astype(jnp.bfloat16), 'replica').astype(jnp.float32)  491 us
    gather x2, local copies, waits for them, and re-layouts, per_device(): slot_grads = jnp.take_along_axis(slot_grad, assignment[:, :, None], axis=1)  334 us
    all_to_all x1, blocking collectives, per_device(): lax.all_to_all(slot_grads, 'group', split_axis=1, concat_axis=0, tiled=True)  277 us
    all_to_all x1, blocking collectives, per_device(): lax.all_to_all(slot_rows, 'group', split_axis=1, concat_axis=0, tiled=True)  271 us
    all_to_all x1, waiting for transfers between devices, per_device(): lax.all_to_all(row_grads, 'group', split_axis=0, concat_axis=1, tiled=True)  269 us
    all_gather x1, blocking collectives, per_device(): lax.all_gather(router, 'group', axis=0, tiled=True)  260 us
    gather x1, local copies, waits for them, and re-layouts, per_device(): jnp.take_along_axis(post_lowered, source_row[:, :, None], axis=1)  178 us
    gather x2, local copies, waits for them, and re-layouts, per_device(): jnp.take_along_axis(flat_out, slot_index[:, :, None], axis=1)  172 us
  transfers between devices with their start and end apart: 16, of which 7 were waited for; matrix products, arithmetic and copies ran while one was open for 15% of the time, Pallas kernels for 0%

commit v1 on v0

v1 whole, which is shorter than its diff:
```python
import functools
import math

import jax
import jax.numpy as jnp
from jax import lax
from jax.experimental import pallas as pl
from jax.experimental.pallas import tpu as pltpu
from jax.sharding import PartitionSpec as P

QUERY_HEADS = 16
KEY_VALUE_HEADS = 8
HEAD_SIZE = 64
E = 32
TOPK = 8
EPSILON = 1e-06
ROPE_BASE = 10000.0
LANES = 128
VMEM_BYTES = 58 * 1024 * 1024

BF = jnp.bfloat16
F32 = jnp.float32
I32 = jnp.int32


def mm(a, b):
    return lax.dot_general(a, b, (((1,), (0,)), ((), ())), preferred_element_type=F32)


def mm_nt(a, b):
    return lax.dot_general(a, b, (((1,), (1,)), ((), ())), preferred_element_type=F32)


def mm_tn(a, b):
    return lax.dot_general(a, b, (((0,), (0,)), ((), ())), preferred_element_type=F32)


def shape(dims, dtype):
    return jax.ShapeDtypeStruct(dims, dtype)


def call(kernel, grid, in_specs, out_specs, out_shape, scratch=(), prefetch=0, flops=0, nbytes=0, aliases=None):
    return pl.pallas_call(
        kernel,
        grid_spec=pltpu.PrefetchScalarGridSpec(
            num_scalar_prefetch=prefetch,
            grid=grid,
            in_specs=in_specs,
            out_specs=out_specs,
            scratch_shapes=list(scratch),
        ),
        out_shape=out_shape,
        input_output_aliases=aliases or {},
        compiler_params=pltpu.CompilerParams(vmem_limit_bytes=VMEM_BYTES),
        cost_estimate=pl.CostEstimate(flops=int(flops), bytes_accessed=int(nbytes), transcendentals=0),
    )


def row_block(rows, most=272):
    best = 16
    for size in range(16, most + 1, 16):
        if rows % size == 0:
            best = size
    return best


def swap_bit(value, axis, bit, size):
    return lax.ppermute(value, axis, [(i, i ^ bit) for i in range(size)])


def gather_relative(value, axis, size, order):
    have = {0: value}
    for bit in order:
        have.update({j ^ bit: swap_bit(held, axis, bit, size) for j, held in list(have.items())})
    return [have[j] for j in range(size)]


def scatter_relative(blocks, axis, size, order):
    have = dict(enumerate(blocks))
    for bit in order:
        for j in [j for j in have if j & bit]:
            arrived = swap_bit(have.pop(j), axis, bit, size)
            kept = have[j ^ bit].astype(F32) + arrived.astype(F32)
            have[j ^ bit] = kept.astype(BF)
    return have[0]


def place(blocks, me):
    count = blocks[0].shape[0]
    whole = jnp.zeros((count * len(blocks),) + blocks[0].shape[1:], blocks[0].dtype)
    for j, block in enumerate(blocks):
        start = ((me ^ j) * count,) + (0,) * (block.ndim - 1)
        whole = lax.dynamic_update_slice(whole, block, start)
    return whole


def rms(values):
    return lax.rsqrt(jnp.mean(values * values, axis=-1, keepdims=True) + EPSILON)


def lane_index():
    return lax.broadcasted_iota(I32, (1, LANES), 1)


def head_ones():
    row = lax.broadcasted_iota(I32, (LANES, LANES), 0) // HEAD_SIZE
    col = lax.broadcasted_iota(I32, (LANES, LANES), 1) // HEAD_SIZE
    return jnp.where(row == col, 1.0 / HEAD_SIZE, 0.0).astype(BF)


def head_mean(values, ones):
    high = values.astype(BF)
    low = (values - high.astype(F32)).astype(BF)
    return mm(high, ones) + mm(low, ones)


def half_swap(values):
    half = HEAD_SIZE // 2
    first = (lane_index() % HEAD_SIZE) < half
    return jnp.where(
        first, pltpu.roll(values, LANES - half, 1), pltpu.roll(values, half, 1)
    )


def project_kernel(x, gain, wq, wk, wv, gq, gk, cos, sin, normed, q_pre, k_pre, q_out, k_out, v_out):
    ones = head_ones()
    values = x[...].astype(F32)
    low = (values * rms(values) * gain[...]).astype(BF)
    normed[...] = low
    q_pre[...] = mm(low, wq[...])
    k_pre[...] = mm(low, wk[...])
    v_out[...] = mm(low, wv[...]).astype(BF)
    for pre, gains, out, factor in ((q_pre, gq, q_out, HEAD_SIZE**-0.5), (k_pre, gk, k_out, 1.0)):
        for start in range(0, pre.shape[1], LANES):
            block = pre[:, start : start + LANES]
            scale = lax.rsqrt(head_mean(block * block, ones) + EPSILON)
            block = block * scale * gains[...]
            turned = block * cos[...] + half_swap(block) * sin[...]
            out[:, start : start + LANES] = (turned * factor).astype(BF)


def project(x, gain, wq, wk, wv, gq, gk, cos, sin):
    rows, width = x.shape
    block = row_block(rows)
    qw, kw = wq.shape[1], wk.shape[1]

    def rowwise(columns):
        return pl.BlockSpec((block, columns), lambda i: (i, 0))

    def whole(array):
        return pl.BlockSpec(array.shape, lambda i: (0,) * array.ndim)

    return call(
        project_kernel,
        (rows // block,),
        [rowwise(width)] + [whole(a) for a in (gain, wq, wk, wv, gq, gk)] + [rowwise(LANES)] * 2,
        [rowwise(c) for c in (width, qw, kw, qw, kw, kw)],
        [
            shape((rows, width), BF),
            shape((rows, qw), F32),
            shape((rows, kw), F32),
            shape((rows, qw), BF),
            shape((rows, kw), BF),
            shape((rows, kw), BF),
        ],
        flops=2 * rows * width * (qw + 2 * kw),
        nbytes=rows * (2 * width + 8 * qw + 14 * kw),
    )(x, gain, wq, wk, wv, gq, gk, cos, sin)


def head_back(pre, gain, incoming, ones, cos, sin):
    turned = incoming * cos - half_swap(incoming) * sin
    scale = lax.rsqrt(head_mean(pre * pre, ones) + EPSILON)
    weighted = turned * gain
    inner = head_mean(weighted * pre, ones)
    grad = scale * weighted - pre * (scale * scale * scale) * inner
    return grad.astype(BF), jnp.sum(turned * pre * scale, axis=0, keepdims=True)


def project_back_kernel(
    dq, dk, dv, q_pre, k_pre, x, normed, grad_middle, gain, wq, wk, wv, gq, gk, cos, sin,
    tokens_grad, dwq, dwk, dwv, d_gain, d_gq, d_gk,
    low_q, low_k, acc_q, acc_k, acc_v,
):
    step = pl.program_id(0)

    @pl.when(step == 0)
    def _():
        for ref in (acc_q, acc_k, acc_v, d_gain, d_gq, d_gk):
            ref[...] = jnp.zeros_like(ref)

    ones = head_ones()
    for incoming, pre, gains, low, total, factor in (
        (dq, q_pre, gq, low_q, d_gq, HEAD_SIZE**-0.5),
        (dk, k_pre, gk, low_k, d_gk, 1.0),
    ):
        for start in range(0, pre.shape[1], LANES):
            span = slice(start, start + LANES)
            grad, terms = head_back(
                pre[:, span], gains[...], incoming[:, span] * factor, ones, cos[...], sin[...]
            )
            low[:, span] = grad
            total[...] += terms
    low_v = dv[...].astype(BF)
    grad_normed = mm_nt(low_q[...], wq[...]) + mm_nt(low_k[...], wk[...]) + mm_nt(low_v, wv[...])
    values = x[...].astype(F32)
    scale = rms(values)
    weighted = grad_normed * gain[...]
    inner = jnp.mean(weighted * values, axis=-1, keepdims=True)
    tokens_grad[...] = (
        grad_middle[...] + scale * weighted - values * (scale * scale * scale) * inner
    ).astype(BF)
    d_gain[...] += jnp.sum(grad_normed * values * scale, axis=0, keepdims=True)
    rows = normed[...]
    acc_q[...] += mm_tn(rows, low_q[...])
    acc_k[...] += mm_tn(rows, low_k[...])
    acc_v[...] += mm_tn(rows, low_v)

    @pl.when(step == pl.num_programs(0) - 1)
    def _():
        dwq[...] = acc_q[...].astype(BF)
        dwk[...] = acc_k[...].astype(BF)
        dwv[...] = acc_v[...].astype(BF)


def project_back(dq, dk, dv, q_pre, k_pre, x, normed, grad_middle, gain, wq, wk, wv, gq, gk, cos, sin):
    rows, width = x.shape
    block = row_block(rows)
    qw, kw = wq.shape[1], wk.shape[1]

    def rowwise(array):
        return pl.BlockSpec((block, array.shape[1]), lambda i: (i, 0))

    def whole(array):
        return pl.BlockSpec(array.shape, lambda i: (0,) * len(array.shape))

    outs = [
        shape((rows, width), BF),
        shape(wq.shape, BF),
        shape(wk.shape, BF),
        shape(wv.shape, BF),
        shape((1, width), F32),
        shape((1, LANES), F32),
        shape((1, LANES), F32),
    ]
    return call(
        project_back_kernel,
        (rows // block,),
        [rowwise(a) for a in (dq, dk, dv, q_pre, k_pre, x, normed, grad_middle)]
        + [whole(a) for a in (gain, wq, wk, wv, gq, gk)]
        + [rowwise(a) for a in (cos, sin)],
        [rowwise(outs[0])] + [whole(a) for a in outs[1:]],
        outs,
        scratch=[
            pltpu.VMEM((block, qw), BF),
            pltpu.VMEM((block, kw), BF),
            pltpu.VMEM(wq.shape, F32),
            pltpu.VMEM(wk.shape, F32),
            pltpu.VMEM(wv.shape, F32),
        ],
        flops=4 * rows * width * (qw + 2 * kw),
        nbytes=rows * (10 * width + 8 * qw + 16 * kw),
    )(dq, dk, dv, q_pre, k_pre, x, normed, grad_middle, gain, wq, wk, wv, gq, gk, cos, sin)


def doubled(block, head):
    values = block.astype(F32)
    keep = (lane_index() // HEAD_SIZE) == (head % 2)
    return jnp.where(keep, values, pltpu.roll(values, HEAD_SIZE, 1)).astype(BF)


def stacked(block):
    low = jnp.where(lane_index() < HEAD_SIZE, 1.0, 0.0).astype(BF)
    high = jnp.where(lane_index() < HEAD_SIZE, 0.0, 1.0).astype(BF)
    return jnp.concatenate([block * low, block * high], axis=0)


def unstacked(values):
    count = values.shape[0] // 2
    return jnp.where(lane_index() < HEAD_SIZE, values[:count], values[count:])


def raised_scores(queries, keys, first, place_of):
    scores = mm_nt(queries, keys)
    columns = lax.broadcasted_iota(I32, scores.shape, 1)
    first = jnp.concatenate([first, first], axis=0)
    place_of = jnp.concatenate([place_of, place_of], axis=0)
    return jnp.where((columns >= first) & (columns <= place_of), jnp.exp(scores), 0.0)


def query_blocks(rows, size=128):
    return [(start, min(size, rows - start)) for start in range(0, rows, size)]


def attend_kernel(causal, q, k, v, first, place_of, out, keys, values):
    head = pl.program_id(0)
    keys[...] = doubled(k[...], head)
    values[...] = doubled(v[...], head)
    for start, count in query_blocks(q.shape[0]):
        span = slice(start, start + count)
        end = start + count if causal else keys.shape[0]
        raised = raised_scores(stacked(q[span, :]), keys[:end, :], first[span, :], place_of[span, :])
        total = jnp.sum(raised, axis=-1, keepdims=True)
        summed = mm(raised.astype(BF), values[:end, :])
        out[span, :] = unstacked(summed * (1.0 / total)).astype(BF)


def attend(q, k, v, first, place_of):
    rows, full = q.shape[0], k.shape[0]
    heads = q.shape[1] // LANES
    qspec = pl.BlockSpec((rows, LANES), lambda j: (0, j))
    kspec = pl.BlockSpec((full, LANES), lambda j: (0, j // 2))
    column = pl.BlockSpec((rows, 1), lambda j: (0, 0))
    return call(
        functools.partial(attend_kernel, rows == full),
        (heads,),
        [qspec, kspec, kspec, column, column],
        qspec,
        shape(q.shape, BF),
        scratch=[pltpu.VMEM((full, LANES), BF)] * 2,
        flops=4 * rows * full * q.shape[1],
        nbytes=4 * q.size + 4 * k.size,
    )(q, k, v, first, place_of)


def attend_back_kernel(causal, q, k, v, grad, first, place_of, dq, dk, dv, keys, values, acc_k, acc_v):
    head = pl.program_id(0)
    keys[...] = doubled(k[...], head)
    values[...] = doubled(v[...], head)
    acc_k[...] = jnp.zeros_like(acc_k)
    acc_v[...] = jnp.zeros_like(acc_v)
    for start, count in query_blocks(q.shape[0]):
        span = slice(start, start + count)
        end = start + count if causal else keys.shape[0]
        queries = stacked(q[span, :])
        grads = stacked(grad[span, :])
        raised = raised_scores(queries, keys[:end, :], first[span, :], place_of[span, :])
        probs = raised * (1.0 / jnp.sum(raised, axis=-1, keepdims=True))
        grad_probs = mm_nt(grads, values[:end, :])
        inner = jnp.sum(probs * grad_probs, axis=-1, keepdims=True)
        grad_scores = (probs * (grad_probs - inner)).astype(BF)
        dq[span, :] = unstacked(mm(grad_scores, keys[:end, :]))
        acc_k[:end, :] += mm_tn(grad_scores, queries)
        acc_v[:end, :] += mm_tn(probs.astype(BF), grads)
    mine = (lane_index() // HEAD_SIZE) == (head % 2)
    for acc, out in ((acc_k, dk), (acc_v, dv)):
        total = acc[...] + pltpu.roll(acc[...], HEAD_SIZE, 1)
        out[...] = jnp.where(mine, total, out[...])


def attend_back(q, k, v, grad, first, place_of):
    rows, full = q.shape[0], k.shape[0]
    heads = q.shape[1] // LANES
    qspec = pl.BlockSpec((rows, LANES), lambda j: (0, j))
    kspec = pl.BlockSpec((full, LANES), lambda j: (0, j // 2))
    column = pl.BlockSpec((rows, 1), lambda j: (0, 0))
    return call(
        functools.partial(attend_back_kernel, rows == full),
        (heads,),
        [qspec, kspec, kspec, qspec, column, column],
        [qspec, kspec, kspec],
        [shape(q.shape, F32), shape(k.shape, F32), shape(k.shape, F32)],
        scratch=[pltpu.VMEM((full, LANES), BF)] * 2 + [pltpu.VMEM((full, LANES), F32)] * 2,
        flops=10 * rows * full * q.shape[1],
        nbytes=8 * q.size + 12 * k.size,
    )(q, k, v, grad, first, place_of)


def split_low(values):
    high = values.astype(BF)
    return high, (values - high.astype(F32)).astype(BF)


def router_kernel(x, att, wo, gain, router, routes, middle, post_a, post_b, gates):
    mid = x[...].astype(F32) + mm(att[...], wo[...])
    middle[...] = mid
    post = (mid * rms(mid) * gain[...]).astype(BF)
    logits = mm(post, router[...])
    lane = lane_index()
    named = routes[:, 0:1] == lane
    for k in range(1, TOPK):
        named = named | (routes[:, k : k + 1] == lane)
    logits = jnp.where(named, logits, -1e30)
    raised = jnp.where(named, jnp.exp(logits - jnp.max(logits, axis=-1, keepdims=True)), 0.0)
    gate = raised / jnp.sum(raised, axis=-1, keepdims=True)
    gates[...] = gate
    high, low = split_low(gate)
    low = pltpu.roll(low.astype(F32), E, 1).astype(BF)
    half = post_a.shape[1]
    post_a[...] = post[:, :half]
    post_b[:, :half] = post[:, half:]
    post_b[:, half:] = high + low


def route_rows(x, att, wo, gain, router, routes):
    rows, width = x.shape
    block = row_block(rows)
    outs = [
        shape((rows, width), F32),
        shape((rows, width // 2), BF),
        shape((rows, width // 2 + LANES), BF),
        shape((rows, LANES), F32),
    ]

    def rowwise(array):
        return pl.BlockSpec((block, array.shape[1]), lambda i: (i, 0))

    def whole(array):
        return pl.BlockSpec(array.shape, lambda i: (0,) * len(array.shape))

    return call(
        router_kernel,
        (rows // block,),
        [rowwise(x), rowwise(att), whole(wo), whole(gain), whole(router), rowwise(routes)],
        [rowwise(a) for a in outs],
        outs,
        flops=2 * rows * width * width,
        nbytes=rows * width * 12,
    )(x, att, wo, gain, router, routes)


def router_back_kernel(
    middle, back_a, back_b, gates, cot, gain, router, wo, att,
    grad_middle, grad_att, dwo, drouter, d_gain,
    acc_o, acc_r,
):
    step = pl.program_id(0)

    @pl.when(step == 0)
    def _():
        for ref in (acc_o, acc_r, d_gain):
            ref[...] = jnp.zeros_like(ref)

    mid = middle[...]
    scale = rms(mid)
    post = (mid * scale * gain[...]).astype(BF)
    half = back_a.shape[1]
    both = back_b[:, half:].astype(F32)
    grad_gates = both + pltpu.roll(both, LANES - E, 1)
    gate = gates[...]
    inner = jnp.sum(gate * grad_gates, axis=-1, keepdims=True)
    grad_logits = (gate * (grad_gates - inner)).astype(BF)
    grad_post = jnp.concatenate(
        [back_a[...].astype(F32), back_b[:, :half].astype(F32)], axis=1
    ) + mm_nt(grad_logits, router[...])
    weighted = grad_post * gain[...]
    mean = jnp.mean(weighted * mid, axis=-1, keepdims=True)
    total = cot[...].astype(F32) + scale * weighted - mid * (scale * scale * scale) * mean
    grad_middle[...] = total
    low = total.astype(BF)
    grad_att[...] = mm_nt(low, wo[...]).astype(BF)
    acc_o[...] += mm_tn(att[...], low)
    acc_r[...] += mm_tn(post, grad_logits)
    d_gain[...] += jnp.sum(grad_post * mid * scale, axis=0, keepdims=True)

    @pl.when(step == pl.num_programs(0) - 1)
    def _():
        dwo[...] = acc_o[...].astype(BF)
        drouter[...] = acc_r[...].astype(BF)


def route_back(middle, back_a, back_b, gates, cot, gain, router, wo, att):
    rows, width = middle.shape
    block = row_block(rows)
    outs = [
        shape((rows, width), F32),
        shape((rows, width), BF),
        shape(wo.shape, BF),
        shape(router.shape, BF),
        shape((1, width), F32),
    ]

    def rowwise(array):
        return pl.BlockSpec((block, array.shape[1]), lambda i: (i, 0))

    def whole(array):
        return pl.BlockSpec(array.shape, lambda i: (0,) * len(array.shape))

    return call(
        router_back_kernel,
        (rows // block,),
        [rowwise(a) for a in (middle, back_a, back_b, gates, cot)]
        + [whole(a) for a in (gain, router, wo)]
        + [rowwise(att)],
        [rowwise(a) for a in outs[:2]] + [whole(a) for a in outs[2:]],
        outs,
        scratch=[pltpu.VMEM(wo.shape, F32), pltpu.VMEM(router.shape, F32)],
        flops=4 * rows * width * width,
        nbytes=rows * width * 18,
    )(middle, back_a, back_b, gates, cot, gain, router, wo, att)


def slot_matrix(rank, cap):
    slots = lax.broadcasted_iota(I32, (cap, 1), 0).astype(F32)
    parts = [
        jnp.where(rank[e : e + 1, :] == slots, 1.0, 0.0).astype(BF) for e in range(rank.shape[0])
    ]
    return jnp.concatenate(parts, axis=0)


def dispatch_kernel(n_in, piece_of, base, rank, part_a, part_b, *refs):
    gated = n_in > 1
    slots = refs[n_in]
    experts, _, cap, width = slots.shape
    half = part_a.shape[2]
    chosen = slot_matrix(rank[0], cap)
    slots[:, 0, :, :half] = mm(chosen, part_a[0]).astype(BF).reshape(experts, cap, half)
    rest = mm(chosen, part_b[0])
    slots[:, 0, :, half:] = rest[:, : width - half].astype(BF).reshape(experts, cap, width - half)
    if rest.shape[1] > width - half:
        gates = refs[n_in + 1]
        both = rest[:, width - half :]
        lane = lane_index()
        for e in range(experts):
            mine = base[0] + e
            picked = (lane == mine) | (lane == mine + E)
            total = jnp.sum(
                jnp.where(picked, both[e * cap : (e + 1) * cap], 0.0), axis=-1, keepdims=True
            )
            gates[e, 0] = jnp.broadcast_to(total, (cap, LANES))


def dispatch(piece_of, base, rank, part_a, part_b, cap, width, earlier):
    pieces, experts, length = rank.shape
    count = part_a.shape[0]
    gated = part_a.shape[2] + part_b.shape[2] > width

    def token_spec(array):
        return pl.BlockSpec((1,) + array.shape[1:], lambda i, piece_of, base: (i, 0, 0))

    def slot_spec(columns):
        return pl.BlockSpec(
            (experts, 1, cap, columns), lambda i, piece_of, base: (0, piece_of[i], 0, 0)
        )

    outs = [shape((experts, pieces, cap, width), BF)]
    out_specs = [slot_spec(width)]
    if gated:
        outs.append(shape((experts, pieces, cap, LANES), F32))
        out_specs.append(slot_spec(LANES))
    earlier = list(earlier or [])
    return call(
        functools.partial(dispatch_kernel, len(earlier)),
        (count,),
        [
            pl.BlockSpec((1, experts, length), lambda i, piece_of, base: (piece_of[i], 0, 0)),
            token_spec(part_a),
            token_spec(part_b),
        ]
        + [pl.BlockSpec(memory_space=pl.ANY)] * len(earlier),
        out_specs,
        outs,
        prefetch=2,
        aliases={5 + i: i for i in range(len(earlier))},
        flops=2 * count * experts * cap * length * width,
        nbytes=2 * count * width * (length + experts * cap),
    )(piece_of, base, rank, part_a, part_b, *earlier)


def combine_kernel(rank, out_rows, back_rows, gate_rows, out_a, out_b, back_a, back_b):
    experts, _, cap, width = out_rows.shape
    half = out_a.shape[2]
    columns = experts * cap
    col = lax.broadcasted_iota(I32, (1, columns), 1)
    expert_row = lax.broadcasted_iota(I32, (experts, 1), 0)
    spread = jnp.where(col // cap == expert_row, 1.0, 0.0).astype(BF)
    wanted = (col % cap).astype(F32)
    chosen = jnp.where(mm(rank[0].astype(BF), spread) == wanted, 1.0, 0.0).astype(BF)
    flat = out_rows[...].reshape(columns, width)
    summed = mm(chosen, flat).astype(BF)
    out_a[0] = summed[:, :half]
    out_b[0] = summed[:, half:]
    summed = mm(chosen, back_rows[...].reshape(columns, width)).astype(BF)
    back_a[0] = summed[:, :half]
    back_b[0, :, :half] = summed[:, half:]
    back_b[0, :, half:] = mm(chosen, gate_rows[...].reshape(columns, LANES)).astype(BF)


def combine(piece_of, rank, out_rows, back_rows, gate_rows):
    experts, pieces, cap, width = out_rows.shape
    _, length, _ = rank.shape
    count = piece_of.shape[0]
    half = width // 2

    def slot_spec(columns):
        return pl.BlockSpec((experts, 1, cap, columns), lambda i, piece_of: (0, piece_of[i], 0, 0))

    def token_spec(columns):
        return pl.BlockSpec((1, length, columns), lambda i, piece_of: (i, 0, 0))

    widths = [half, half, half, half + LANES]
    return call(
        lambda piece_of, *refs: combine_kernel(*refs),
        (count,),
        [
            pl.BlockSpec((1, length, experts), lambda i, piece_of: (piece_of[i], 0, 0)),
            slot_spec(width),
            slot_spec(width),
            slot_spec(LANES),
        ],
        [token_spec(c) for c in widths],
        [shape((count, length, c), BF) for c in widths],
        prefetch=1,
        flops=4 * count * experts * cap * length * width,
        nbytes=4 * count * width * (length + experts * cap),
    )(piece_of, rank, out_rows, back_rows, gate_rows)


def expert_kernel(n_in, first, base, rows, grads, gates, w_in, w_out, *refs):
    outs, backs, gate_grads, dw_in, dw_out, acc_in, acc_out = refs[n_in:]
    step = pl.program_id(1)
    _, pieces, cap, width = rows.shape
    count = pieces * cap
    hidden_width = w_out.shape[1]

    @pl.when(step == 0)
    def _():
        acc_in[...] = jnp.zeros_like(acc_in)
        acc_out[...] = jnp.zeros_like(acc_out)

    x = rows[...].reshape(count, width)
    grad = grads[...].reshape(count, width)
    gate = gates[...].reshape(count, LANES)[:, 0:1]
    gate_up = mm(x, w_in[0])
    a = gate_up[:, :hidden_width]
    u = gate_up[:, hidden_width:]
    sigma = 1.0 / (1.0 + jnp.exp(-a))
    silu = a * sigma
    hidden = silu * u
    low = hidden.astype(BF)
    outs[...] = (mm(low, w_out[0]) * gate).astype(BF).reshape(outs.shape)
    grad_hidden = mm_nt(grad, w_out[0])
    inner = jnp.sum(low.astype(F32) * grad_hidden, axis=-1, keepdims=True)
    grad_hidden = grad_hidden * gate
    grad_a = grad_hidden * u * (sigma * (1.0 + a * (1.0 - sigma)))
    grad_u = grad_hidden * silu
    grad_gate_up = jnp.concatenate([grad_a, grad_u], axis=1).astype(BF)
    backs[...] = mm_nt(grad_gate_up, w_in[0]).astype(BF).reshape(backs.shape)
    acc_in[...] += mm_tn(x, grad_gate_up)
    acc_out[...] += mm_tn((hidden * gate).astype(BF), grad)
    lane = lane_index()
    mine = base[0] + first + pl.program_id(0)
    high = inner.astype(BF).astype(F32)
    both = jnp.where(lane == mine, high, jnp.where(lane == mine + E, inner - high, 0.0))
    gate_grads[...] = both.astype(BF).reshape(gate_grads.shape)

    @pl.when(step == pl.num_programs(1) - 1)
    def _():
        dw_in[0] = acc_in[...].astype(BF)
        dw_out[0] = acc_out[...].astype(BF)


def run_experts(first, number, base, rows, grads, gates, w_in, w_out, earlier):
    experts, pieces, cap, width = rows.shape
    group = max(1, 384 // cap)
    hidden_width = w_out.shape[1]

    def slot_spec(columns):
        return pl.BlockSpec((1, group, cap, columns), lambda e, c, base: (first + e, c, 0, 0))

    def weight_spec(array, offset):
        return pl.BlockSpec((1,) + array.shape[1:], lambda e, c, base: (offset + e, 0, 0))

    outs = [
        shape(rows.shape, BF),
        shape(rows.shape, BF),
        shape((experts, pieces, cap, LANES), BF),
        shape((number,) + w_in.shape[1:], BF),
        shape((number,) + w_out.shape[1:], BF),
    ]
    earlier = list(earlier or [])
    return call(
        functools.partial(lambda n_in, base, *refs: expert_kernel(n_in, first, base, *refs), len(earlier)),
        (number, pieces // group),
        [slot_spec(width), slot_spec(width), slot_spec(LANES), weight_spec(w_in, first), weight_spec(w_out, first)]
        + [pl.BlockSpec(memory_space=pl.ANY)] * len(earlier),
        [slot_spec(width), slot_spec(width), slot_spec(LANES), weight_spec(outs[3], 0), weight_spec(outs[4], 0)],
        outs,
        scratch=[pltpu.VMEM(w_in.shape[1:], F32), pltpu.VMEM(w_out.shape[1:], F32)],
        prefetch=1,
        aliases={6 + i: i for i in range(len(earlier))},
        flops=18 * number * pieces * cap * width * hidden_width,
        nbytes=number * (8 * pieces * cap * width + 12 * width * hidden_width),
    )(base, rows, grads, gates, w_in, w_out, *earlier)


def per_device(
    tokens, segments, routes, norm_in, q_weight, key_weight, value_weight, q_gain, k_gain,
    o_weight, norm_post, router, expert_in, expert_out, cotangent,
):
    size = lax.axis_size("group")
    me = lax.axis_index("group")
    sequences, length, width = tokens.shape
    half = width // 2
    parts = size // sequences
    rows = sequences * length
    full = length * size
    experts = expert_in.shape[0]
    cap = (length * TOPK * 4 // (3 * E) + 7) // 8 * 8
    bits = [1 << b for b in range(size.bit_length() - 1)]
    order_a, order_b = bits, bits[::-1]
    part, sequence = me // sequences, me % sequences
    exchange = [[q * sequences + s for s in range(sequences)] for q in range(parts)]
    fellows = [[q * sequences + s for q in range(parts)] for s in range(sequences)]

    def regroup(value):
        return lax.all_to_all(
            value, "group", 0, 0, tiled=True, axis_index_groups=exchange if parts > 1 else None
        )

    def gathered(value, order):
        return gather_relative(value, "group", size, order)

    x = regroup(tokens).reshape(rows, width)
    kv_weight = jnp.concatenate([key_weight, value_weight], axis=1)
    wq = place(gathered(q_weight, order_a), me)
    wkv = place(gathered(kv_weight, order_b), me)
    key_width = key_weight.shape[1]
    wk, wv = wkv[:, :key_width], wkv[:, key_width:]
    small = jnp.concatenate([norm_in, norm_post, q_gain, k_gain])
    small = lax.all_gather(small, "group").astype(F32)
    n_norm, n_gain = norm_in.shape[0], q_gain.shape[0]
    cuts = [0, n_norm, 2 * n_norm, 2 * n_norm + n_gain, 2 * n_norm + 2 * n_gain]
    gain_in, gain_post, gain_q, gain_k = (
        small[:, a:b].reshape(1, -1) for a, b in zip(cuts[:-1], cuts[1:])
    )
    gain_q = jnp.concatenate([gain_q, gain_q], axis=1)
    gain_k = jnp.concatenate([gain_k, gain_k], axis=1)

    seg_all = lax.all_gather(segments, "group", axis=1, tiled=True)
    seg_full = lax.dynamic_index_in_dim(seg_all, sequence, 0, keepdims=False)
    place_of = part * rows + jnp.arange(rows, dtype=I32)
    seg_own = lax.dynamic_slice_in_dim(seg_full, part * rows, rows)
    first = jnp.sum((seg_full[None, :] < seg_own[:, None]).astype(I32), axis=1)
    frequency = jnp.exp(
        -(2.0 * jnp.arange(HEAD_SIZE // 2, dtype=F32) / HEAD_SIZE) * math.log(ROPE_BASE)
    )
    phase = (place_of - first).astype(F32)[:, None] * frequency
    cos, sin = jnp.cos(phase), jnp.sin(phase)
    cos = jnp.concatenate([cos] * 4, axis=1)
    sin = jnp.concatenate([-sin, sin, -sin, sin], axis=1)
    first, place_of = first[:, None], place_of[:, None]

    routes_all = lax.all_gather(routes, "group")
    pieces = size * sequences
    base = me * experts
    local = routes_all.reshape(pieces, length, TOPK) - base
    hit = jnp.zeros((pieces, length, experts), jnp.bool_)
    for k in range(TOPK):
        hit = hit | (local[:, :, k : k + 1] == jnp.arange(experts, dtype=I32))
    before = (jnp.arange(length)[:, None] > jnp.arange(length)[None, :]).astype(BF)
    rank = jnp.einsum("ij,pje->pie", before, hit.astype(BF), preferred_element_type=F32)
    rank = jnp.where(hit, rank, -1.0)
    rank_rows = rank.transpose(0, 2, 1)
    base = base.reshape(1)
    own_routes = lax.dynamic_slice(
        routes_all, (part * sequences, sequence, 0, 0), (sequences, 1, length, TOPK)
    ).reshape(rows, TOPK)

    def sequence_pieces(j):
        other = me ^ j
        return (other // sequences * sequences + jnp.arange(sequences, dtype=I32)) * sequences + other % sequences

    def position_pieces(j):
        return (me ^ j) * sequences + jnp.arange(sequences, dtype=I32)

    cot_a = gathered(cotangent[:, :, :half], order_a)
    cot_b = gathered(cotangent[:, :, half:], order_b)

    normed, q_pre, k_pre, queries, keys, values = project(
        x, gain_in, wq, wk, wv, gain_q, gain_k, cos, sin
    )
    if parts > 1:
        keys = lax.all_gather(keys, "group", axis=0, tiled=True, axis_index_groups=fellows)
        values = lax.all_gather(values, "group", axis=0, tiled=True, axis_index_groups=fellows)
    attended = attend(queries, keys, values, first, place_of)

    wo_router = jnp.concatenate(
        [o_weight, router, jnp.zeros((router.shape[0], LANES - E), BF)], axis=1
    )
    wo = jnp.concatenate(
        [
            place(gathered(wo_router[:, :half], order_a), me),
            place(gathered(wo_router[:, half:], order_b), me),
        ],
        axis=1,
    )
    wo, router_full = wo[:, :width], wo[:, width:]
    middle, post_a, post_b, gates = route_rows(x, attended, wo, gain_post, router_full, own_routes)

    slot_grads = None
    for j in range(size):
        slot_grads = dispatch(
            position_pieces(j), base, rank_rows, cot_a[j], cot_b[j], cap, width, slot_grads
        )
    posts_a = gathered(post_a.reshape(sequences, length, -1), order_a)
    posts_b = gathered(post_b.reshape(sequences, length, -1), order_b)
    slot_rows = None
    for j in range(size):
        slot_rows = dispatch(
            sequence_pieces(j), base, rank_rows, posts_a[j], posts_b[j], cap, width, slot_rows
        )
    made = None
    grads_in, grads_out = [], []
    step = 2 if experts % 2 == 0 else 1
    for e in range(0, experts, step):
        *made, grad_in, grad_out = run_experts(
            e, step, base, slot_rows[0], slot_grads[0], slot_rows[1], expert_in, expert_out, made
        )
        grads_in.append(lax.psum(grad_in, "replica").astype(F32))
        grads_out.append(lax.psum(grad_out, "replica").astype(F32))
    expert_in_grad = jnp.concatenate(grads_in, axis=0)
    expert_out_grad = jnp.concatenate(grads_out, axis=0)

    combined = [combine(sequence_pieces(j), rank, *made) for j in range(size)]
    out_a, out_b, back_a, back_b = (
        scatter_relative([c[i] for c in combined], "group", size, order).reshape(rows, -1)
        for i, order in ((0, order_a), (1, order_b), (2, order_a), (3, order_b))
    )
    summed = jnp.concatenate([out_a, out_b], axis=1).astype(F32)
    layer_out = regroup((middle + summed).astype(BF).reshape(sequences, length, width))

    own_cot = []
    for cot in (cot_a, cot_b):
        stack = jnp.stack([lax.dynamic_index_in_dim(c, sequence, 0, keepdims=False) for c in cot])
        own_cot.append(
            jnp.concatenate(
                [
                    lax.dynamic_index_in_dim(stack, (part * sequences + i) ^ me, 0, keepdims=False)
                    for i in range(sequences)
                ],
                axis=0,
            )
        )
    own_cot = jnp.concatenate(own_cot, axis=1)
    grad_middle, grad_att, dwo, drouter, d_norm_post = route_back(
        middle, back_a, back_b, gates, own_cot, gain_post, router_full, wo, attended
    )
    dq, dk, dv = attend_back(queries, keys, values, grad_att, first, place_of)
    if parts > 1:
        dk, dv = (
            lax.psum_scatter(
                d.astype(BF), "group", scatter_dimension=0, tiled=True, axis_index_groups=fellows
            ).astype(F32)
            for d in (dk, dv)
        )
    tokens_grad, dwq, dwk, dwv, d_norm_in, d_gq, d_gk = project_back(
        dq, dk, dv, q_pre, k_pre, x, normed, grad_middle, gain_in, wq, wk, wv, gain_q, gain_k, cos, sin
    )
    tokens_grad = regroup(tokens_grad.reshape(sequences, length, width)).astype(F32)

    big = jnp.concatenate([dwq, dwk, dwv, dwo, drouter], axis=1)
    big = lax.psum_scatter(big, "group", scatter_dimension=0, tiled=True)
    big = lax.psum(big, "replica").astype(F32)
    cuts = [0]
    for piece in (dwq, dwk, dwv, dwo):
        cuts.append(cuts[-1] + piece.shape[1])
    cuts.append(cuts[-1] + E)
    shard_q, shard_k, shard_v, shard_o, shard_router = (
        big[:, a:b] for a, b in zip(cuts[:-1], cuts[1:])
    )
    d_gq = d_gq[:, :HEAD_SIZE] + d_gq[:, HEAD_SIZE:]
    d_gk = d_gk[:, :HEAD_SIZE] + d_gk[:, HEAD_SIZE:]
    vectors = jnp.concatenate([d_norm_in, d_norm_post, d_gq, d_gk], axis=1)[0]
    vectors = lax.psum(vectors, ("group", "replica"))

    def own_part(start, count):
        return lax.dynamic_slice_in_dim(vectors, start + me * (count // size), count // size)

    return (
        layer_out,
        tokens_grad,
        own_part(0, width),
        shard_q,
        shard_k,
        shard_v,
        own_part(2 * width, HEAD_SIZE),
        own_part(2 * width + HEAD_SIZE, HEAD_SIZE),
        shard_o,
        own_part(width, width),
        shard_router,
        expert_in_grad,
        expert_out_grad,
    )


def solution(mesh):
    row, column = P("group", None), P("group")
    stream = P("replica", "group", None)
    expert = P("group", None, None)
    return jax.shard_map(
        per_device,
        mesh=mesh,
        in_specs=(
            stream, P("replica", "group"), stream, column, row, row, row, column, column,
            row, column, row, expert, expert, stream,
        ),
        out_specs=(
            stream, stream, column, row, row, row, column, column, row, column, row, expert, expert,
        ),
        check_vma=False,
    )
```

time: 4050 us -> 1380 us (0.34)
  local copies, waits for them, and re-layouts: 1260 us -> 63.1 us
  blocking collectives: 881 us -> 140 us
  matrix products: 526 us -> 10.1 us
  Pallas kernels: 0 us -> 435 us
  other arithmetic: 452 us -> 76.3 us
  waiting for transfers between devices: 865 us -> 581 us
    gather x11 -> x0, local copies, waits for them, and re-layouts: 939 us -> none  [the longest x2 334 us: per_device(): slot_grads = jnp.take_along_axis(slot_grad, assignment[:, :, None], axis=1)]
    all_to_all x2 -> x1, blocking collectives: 548 us -> 26.8 us  [regroup(): lax.all_to_all(value, 'group', 0, 0, tiled=True, axis_index_groups=exchan...]
    dot_general x77 -> x1, matrix products: 526 us -> 10.1 us  [per_device(): jnp.einsum('ij,pje->pie', before, hit.astype(BF), preferred_element_type=...]
    pallas_call x0 -> x22, Pallas kernels: none -> 435 us  [the longest x4 174 us: run_experts(): call(functools.partial(lambda n_in, base, *refs: expert_kernel(n_in, firs...]
    all_gather x4 -> x2, blocking collectives: 285 us -> 15.9 us  [the longest x1 8.72 us: per_device(): routes_all = lax.all_gather(routes, 'group')]
    all_to_all x2, waiting for transfers between devices: 269 us -> 0.01 us  [regroup(): lax.all_to_all(value, 'group', 0, 0, tiled=True, axis_index_groups=exchan...]
    ppermute x0 -> x36, waiting for transfers between devices: none -> 149 us  [swap_bit(): return lax.ppermute(value, axis, [(i, i ^ bit) for i in range(size)])]
    convert_element_type x30 -> x11, other arithmetic: 160 us -> 14.7 us  [the longest x8 9.7 us: scatter_relative(): have[j ^ bit] = kept.astype(BF)]
  transfers between devices with their start and end apart: 16 -> 40, of which waited for: 7 -> 15; matrix products, arithmetic and copies ran while one was open for 15% -> 7% of each run, Pallas kernels for 0% -> 10%
where the time goes in v1:
time: 1380 us; the launch traced here: 1370 us
  waiting for transfers between devices  581 us (42%)
  Pallas kernels  435 us (32%)
  blocking collectives  140 us (10%)
  other arithmetic  76.3 us (6%)
  local copies, waits for them, and re-layouts  63.1 us (5%)
  starting transfers between devices  48.3 us (4%)
  between operations  16.1 us (1%)
    psum x1, waiting for transfers between devices, per_device(): big = lax.psum(big, 'replica').astype(F32)  360 us
    pallas_call x4, Pallas kernels, run_experts(): call(functools.partial(lambda n_in, base, *refs: expert_kernel(n_in, firs...  174 us
    ppermute x36, waiting for transfers between devices, swap_bit(): return lax.ppermute(value, axis, [(i, i ^ bit) for i in range(size)])  149 us
    reduce_scatter x1, waiting for transfers between devices, per_device(): big = lax.psum_scatter(big, 'group', scatter_dimension=0, tiled=True)  72.8 us
    pallas_call x8, Pallas kernels, dispatch(): call(functools.partial(dispatch_kernel, len(earlier)), (count,), [pl.Bloc...  63.3 us
    pallas_call x1, Pallas kernels, attend_back(): call(functools.partial(attend_back_kernel, rows == full), (heads,), [qspe...  62.1 us
    psum x1, blocking collectives, per_device(): vectors = lax.psum(vectors, ('group', 'replica'))  57.2 us
    unnamed x1, blocking collectives  40.1 us
  transfers between devices with their start and end apart: 40, of which 15 were waited for; matrix products, arithmetic and copies ran while one was open for 7% of the time, Pallas kernels for 10%

profile of v1, /device:TPU:0, one launch (start us, length us, event | category | flops | bytes accessed | tf_op | source)
XLA Modules:
  0.0 1370.1 jit_solution(159305107416115513)
XLA Ops:
  24.6 40.1 %all-reduce = bf16[2176]{0:T(1024)(128)(2,1)S(1)} all-reduce(bf16[2176]{0:T(1024)(128)(2,1)S(1)} %dynamic-update-slice), channel_id=2, replica_groups=mesh['group'=4,'replica'=8] {'group'}, use_global_device_ids=true, to_apply=%add | all-reduce | flops 2176 | bytes 8704
  94.8 10.1 fusion.18
  134.9 28.2 %collective-permute-done.8 = bf16[256,512]{1,0:T(8,128)(2,1)S(1)} collective-permute-done((bf16[256,512]{1,0:T(8,128)(2,1)}, bf16[256,512]{1,0:T(8,128)(2,1)S(1)}, u32[]{:S(2)}, u32[]{:S(2)}) %collective-permute-start.8) | collective-permute-done | bytes 262176 | tf_op jit(solution)/shard_map/ppermute | solution.py:68
  181.7 13.4 shard_map.246
  195.1 24.6 %shard_map.247.att = bf16[1088,1024]{1,0:T(8,128)(2,1)} custom-call(bf16[1088,1024]{1,0:T(8,128)(2,1)} %get-tuple-element.82.q, bf16[1088,512]{1,0:T(8,128)(2,1)} %get-tuple-element.83.k, bf16[1088,512]{1,0:T(8,128)(2,1)} %get-tuple-element.84.v, s32[1088,1]{1,0:T(8,128)} %reduce_sum.13.first, s32[1088,1]{1,0:T(8,128)} %iota_add_fusion.place_of), custom_call_target="tpu_custom_call" | custom-call | flops 4848615424 | bytes 6684672 | tf_op jit(solution)/shard_map/pallas_call | solution.py:314
  270.8 20.6 %collective-permute-done.12.part_a = bf16[4,272,512]{2,1,0:T(8,128)(2,1)} collective-permute-done((bf16[4,272,512]{2,1,0:T(8,128)(2,1)}, bf16[4,272,512]{2,1,0:T(8,128)(2,1)}, u32[]{:S(2)}, u32[]{:S(2)}) %collective-permute-start.12) | collective-permute-done | bytes 1114144 | tf_op jit(solution)/shard_map/ppermute | solution.py:68
  348.1 43.4 %shard_map.257 = (bf16[8,16,96,1024]{3,2,1,0:T(8,128)(2,1)}, bf16[8,16,96,1024]{3,2,1,0:T(8,128)(2,1)}, bf16[8,16,96,128]{3,2,1,0:T(8,128)(2,1)}, bf16[2,1024,1024]{2,1,0:T(8,128)(2,1)}, bf16[2,512,1024]{2,1,0:T(8,128)(2,1)}) custom-call(s32[1]{0:T(128)} %bitcast.17.base, bf16[8,16,96,1024]{3,2,1,0:T(8,128)(2,1)} %get-tuple-element.94.refs_0_, ...), custom_call_target="tpu_custom_call" | custom-call | flops 28991029248 | bytes 37748736 | tf_op jit(solution)/shard_map/pallas_call | solution.py:672
  391.5 43.6 %shard_map.258 = (bf16[8,16,96,1024]{3,2,1,0:T(8,128)(2,1)}, bf16[8,16,96,1024]{3,2,1,0:T(8,128)(2,1)}, bf16[8,16,96,128]{3,2,1,0:T(8,128)(2,1)}, bf16[2,1024,1024]{2,1,0:T(8,128)(2,1)}, bf16[2,512,1024]{2,1,0:T(8,128)(2,1)}) custom-call(s32[1]{0:T(128)} %bitcast.17.base, ...), custom_call_target="tpu_custom_call", output_to_operand_aliasing={{0}: (6, {}), {1}: (7, {}), {2}: (8, {})} | custom-call | flops 28991029248 | bytes 37748736 | tf_op jit(solution)/shard_map/pallas_call | solution.py:672
  435.1 43.4 %shard_map.259 = (bf16[8,16,96,1024]{3,2,1,0:T(8,128)(2,1)}, bf16[8,16,96,1024]{3,2,1,0:T(8,128)(2,1)}, bf16[8,16,96,128]{3,2,1,0:T(8,128)(2,1)}, bf16[2,1024,1024]{2,1,0:T(8,128)(2,1)}, bf16[2,512,1024]{2,1,0:T(8,128)(2,1)}) custom-call(s32[1]{0:T(128)} %bitcast.17.base, ...), custom_call_target="tpu_custom_call", output_to_operand_aliasing={{0}: (6, {}), {1}: (7, {}), {2}: (8, {})} | custom-call | flops 28991029248 | bytes 37748736 | tf_op jit(solution)/shard_map/pallas_call | solution.py:672
  478.6 43.9 %shard_map.260 = (bf16[8,16,96,1024]{3,2,1,0:T(8,128)(2,1)}, bf16[8,16,96,1024]{3,2,1,0:T(8,128)(2,1)}, bf16[8,16,96,128]{3,2,1,0:T(8,128)(2,1)}, bf16[2,1024,1024]{2,1,0:T(8,128)(2,1)}, bf16[2,512,1024]{2,1,0:T(8,128)(2,1)}) custom-call(s32[1]{0:T(128)} %bitcast.17.base, ...), custom_call_target="tpu_custom_call", output_to_operand_aliasing={{0}: (6, {}), {1}: (7, {}), {2}: (8, {})} | custom-call | flops 28991029248 | bytes 37748736 | tf_op jit(solution)/shard_map/pallas_call | solution.py:672
  522.5 9.9 shard_map.264
  536.6 9.9 shard_map.263
  568.7 14.3 %maximum_maximum_fusion.cot = bf16[1088,1024]{1,0:T(8,128)(2,1)} fusion(bf16[272,512]{1,0:T(8,128)(2,1)S(1)} %get-tuple-element.238, bf16[272,512]{1,0:T(8,128)(2,1)S(1)} %get-tuple-element.239, bf16[272,512]{1,0:T(8,128)(2,1)S(1)} %get-tuple-element.240, bf16[272,512]{1,0:T(8,128)(2,1)S(1)} %get-tuple-element.237, ...), kind=kLoop, calls=%fused_computation.7 | loop fusion | flops 17825792 | bytes 4456448 | tf_op jit(solution)/shard_map/concatenate | solution.py:835
  606.1 17.2 %shard_map.265 = (f32[1088,1024]{1,0:T(8,128)}, bf16[1088,1024]{1,0:T(8,128)(2,1)}, bf16[1024,1024]{1,0:T(8,128)(2,1)}, bf16[1024,128]{1,0:T(8,128)(2,1)}, f32[1,1024]{1,0:T(1,128)}) custom-call(f32[1088,1024]{1,0:T(8,128)} %get-tuple-element.85.middle, bf16[1088,512]{1,0:T(8,128)(2,1)} %bitcast.78, bf16[1088,640]{1,0:T(8,128)(2,1)} %bitcast.77, ...), custom_call_target="tpu_custom_call" | custom-call | flops 4563402752 | bytes 20054016 | tf_op jit(solution)/shard_map/pallas_call | solution.py:479
  623.3 62.1 %shard_map.266 = (f32[1088,1024]{1,0:T(8,128)}, f32[1088,512]{1,0:T(8,128)}, f32[1088,512]{1,0:T(8,128)}) custom-call(bf16[1088,1024]{1,0:T(8,128)(2,1)} %get-tuple-element.82.q, bf16[1088,512]{1,0:T(8,128)(2,1)} %get-tuple-element.83.k, bf16[1088,512]{1,0:T(8,128)(2,1)} %get-tuple-element.84.v, bf16[1088,1024]{1,0:T(8,128)(2,1)} %get-tuple-element.125.grad, ...), custom_call_target="tpu_custom_call" | custom-call | flops 12121538560 | bytes 15597568 | tf_op jit(solution)/shard_map/pallas_call | solution.py:357
  685.5 31.2 %shard_map.267 = (bf16[1088,1024]{1,0:T(8,128)(2,1)}, bf16[1024,1024]{1,0:T(8,128)(2,1)}, bf16[1024,512]{1,0:T(8,128)(2,1)}, bf16[1024,512]{1,0:T(8,128)(2,1)}, ...) custom-call(f32[1088,1024]{1,0:T(8,128)} %get-tuple-element.126.dq, f32[1088,512]{1,0:T(8,128)} %get-tuple-element.127.dk, ...), custom_call_target="tpu_custom_call" | custom-call | flops 9126805504 | bytes 28966912 | tf_op jit(solution)/shard_map/pallas_call | solution.py:246
  724.2 72.8 %reduce-scatter.2.cloned.1.call-done = bf16[256,3200]{1,0:T(8,128)(2,1)} async-done(((bf16[1024,3200]{1,0:T(8,128)(2,1)}), bf16[256,3200]{1,0:T(8,128)(2,1)}) %reduce-scatter.2.cloned.1.call-update) | async-done | bytes 1638416 | tf_op jit(solution)/shard_map/reduce_scatter | solution.py:853
  801.6 24.1 %collective-permute-done.28 = bf16[4,272,512]{2,1,0:T(8,128)(2,1)S(1)} collective-permute-done((bf16[4,272,512]{2,1,0:T(8,128)(2,1)S(1)}, bf16[4,272,512]{2,1,0:T(8,128)(2,1)S(1)}, u32[]{:S(2)}, u32[]{:S(2)}) %collective-permute-start.28) | collective-permute-done | bytes 1114144 | tf_op jit(solution)/shard_map/ppermute | solution.py:68
  829.9 19.7 %collective-permute-done.27 = bf16[4,272,512]{2,1,0:T(8,128)(2,1)S(1)} collective-permute-done((bf16[4,272,512]{2,1,0:T(8,128)(2,1)}, bf16[4,272,512]{2,1,0:T(8,128)(2,1)S(1)}, u32[]{:S(2)}, u32[]{:S(2)}) %collective-permute-start.27) | collective-permute-done | bytes 1114144 | tf_op jit(solution)/shard_map/ppermute | solution.py:68
  854.1 20.3 %collective-permute-done.24 = bf16[4,272,512]{2,1,0:T(8,128)(2,1)S(1)} collective-permute-done((bf16[4,272,512]{2,1,0:T(8,128)(2,1)}, bf16[4,272,512]{2,1,0:T(8,128)(2,1)S(1)}, u32[]{:S(2)}, u32[]{:S(2)}) %collective-permute-start.24) | collective-permute-done | bytes 1114144 | tf_op jit(solution)/shard_map/ppermute | solution.py:68
  875.7 26.8 %all_to_all.15 = bf16[4,272,1024]{2,1,0:T(8,128)(2,1)S(1)} all-to-all(bf16[4,272,1024]{2,1,0:T(8,128)(2,1)S(1)} %bitcast.71), channel_id=1, replica_groups=mesh['group'=4,'replica'=8] {'group'}, dimensions={0} | all-to-all | bytes 4456448 | tf_op jit(solution)/shard_map/all_to_all | solution.py:707
  907.4 57.2 %psum.70 = f32[2176]{0:T(1024)S(1)} all-reduce(f32[2176]{0:T(1024)S(1)} %reduce.1), channel_id=1, replica_groups=mesh['group'=4,'replica'=8] {'group','replica'}, use_global_device_ids=true, to_apply=%region_1.2 | all-reduce | flops 2176 | bytes 17408 | tf_op jit(solution)/shard_map/psum | solution.py:865
  970.0 359.8 %all-reduce.4.cloned.1.call-done = (bf16[256,3200]{1,0:T(8,128)(2,1)}, bf16[2,1024,1024]{2,1,0:T(8,128)(2,1)}, bf16[2,1024,1024]{2,1,0:T(8,128)(2,1)}, bf16[2,10...) async-done(((bf16[256,3200]{1,0:T(8,128)(2,1)}, ...) | async-done | bytes 26804240 | tf_op jit(solution)/shard_map/psum | solution.py:854
  1335.2 20.0 %maximum_convert_fusion = f32[8,1024,1024]{2,1,0:T(8,128)} fusion(bf16[2,1024,1024]{2,1,0:T(8,128)(2,1)} %get-tuple-element.217, bf16[2,1024,1024]{2,1,0:T(8,128)(2,1)} %get-tuple-element.218, bf16[2,1024,1024]{2,1,0:T(8,128)(2,1)} %get-tuple-element.219, bf16[2,1024,1024]{2,1,0:T(8,128)(2,1)} %get-tuple-element.220), kind=kLoop, calls=%fused_computation | loop fusion | flops 33554432 | bytes 50331648 | tf_op jit(solution)/shard_map/concatenate | solution.py:812
  (323 shorter events, 297.6 us)
Async XLA Ops:
  7.2 119.2 %collective-permute-start.1 = (bf16[256,1024]{1,0:T(8,128)(2,1)}, bf16[256,1024]{1,0:T(8,128)(2,1)}, u32[]{:S(2)}, u32[]{:S(2)}) collective-permute-start(bf16[256,1024]{1,0:T(8,128)(2,1)} %param.19), channel_id=1, source_target_pairs={{0,16},{8,24},{16,0},{24,8},{1,17},{9,25},{17,1},{25,9},{2,18},{10... | collective-permute-start | bytes 1572872 | tf_op jit(solution)/shard_map/ppermute | solution.py:68
  10.2 112.7 %collective-permute-start = (bf16[256,1024]{1,0:T(8,128)(2,1)}, bf16[256,1024]{1,0:T(8,128)(2,1)}, u32[]{:S(2)}, u32[]{:S(2)}) collective-permute-start(bf16[256,1024]{1,0:T(8,128)(2,1)} %param.19), channel_id=1, source_target_pairs={{0,8},{8,0},{16,24},{24,16},{1,9},{9,1},{17,25},{25,17},{2,10},{10... | collective-permute-start | bytes 1572872 | tf_op jit(solution)/shard_map/ppermute | solution.py:68
  14.5 96.9 %collective-permute-start.6 = (bf16[256,512]{1,0:T(8,128)(2,1)}, bf16[256,512]{1,0:T(8,128)(2,1)}, u32[]{:S(2)}, u32[]{:S(2)}) collective-permute-start(bf16[256,512]{1,0:T(8,128)(2,1)} %get-tuple-element.243), channel_id=1, source_target_pairs={{0,8},{8,0},{16,24},{24,16},{1,9},{9,1},{17,25},{25,17},{2,10},{10... | collective-permute-start | bytes 786440 | tf_op jit(solution)/shard_map/ppermute | solution.py:68
  15.1 98.6 %collective-permute-start.7 = (bf16[256,512]{1,0:T(8,128)(2,1)}, bf16[256,512]{1,0:T(8,128)(2,1)}, u32[]{:S(2)}, u32[]{:S(2)}) collective-permute-start(bf16[256,512]{1,0:T(8,128)(2,1)} %get-tuple-element.243), channel_id=1, source_target_pairs={{0,16},{8,24},{16,0},{24,8},{1,17},{9,25},{17,1},{25,9},{2,18},{10... | collective-permute-start | bytes 786440 | tf_op jit(solution)/shard_map/ppermute | solution.py:68
  15.1 166.6 %all-to-all-start = ((bf16[4,272,1024]{2,1,0:T(8,128)(2,1)}), bf16[4,272,1024]{2,1,0:T(8,128)(2,1)}, u32[]{:S(2)}, u32[]{:S(2)}) async-start(bf16[4,272,1024]{2,1,0:T(8,128)(2,1)} %param.15), calls=%async_computation | async-start | bytes 4456448 | tf_op jit(solution)/shard_map/all_to_all | solution.py:707
  19.7 777.4 %reduce-scatter.2.cloned.1.call-start = ((), (), s32[]{:S(2)}) async-start(), calls=%async_computation.4 | async-start | bytes 8192000 | tf_op jit(solution)/shard_map/reduce_scatter | solution.py:853
  21.1 95.8 %collective-permute-start.9 = (bf16[256,640]{1,0:T(8,128)(2,1)}, bf16[256,640]{1,0:T(8,128)(2,1)}, u32[]{:S(2)}, u32[]{:S(2)}) collective-permute-start(bf16[256,640]{1,0:T(8,128)(2,1)} %get-tuple-element.241), channel_id=1, source_target_pairs={{0,8},{8,0},{16,24},{24,16},{1,9},{9,1},{17,25},{25,17},{2,10},{10... | collective-permute-start | bytes 983048 | tf_op jit(solution)/shard_map/ppermute | solution.py:68
  122.3 119.5 %collective-permute-start.23 = (bf16[4,272,512]{2,1,0:T(8,128)(2,1)}, bf16[4,272,512]{2,1,0:T(8,128)(2,1)}, u32[]{:S(2)}, u32[]{:S(2)}) collective-permute-start(bf16[4,272,512]{2,1,0:T(8,128)(2,1)} %get-tuple-element.225.part_b), channel_id=1, source_target_pairs={{0,8},{8,0},{16,24},{24,16},{1,9},{9,1},{17,25},{25,17},{2,10},{10... | collective-permute-start | bytes 3342344 | tf_op jit(solution)/shard_map/ppermute | solution.py:68
  122.9 116.8 %collective-permute-start.20 = (bf16[4,272,512]{2,1,0:T(8,128)(2,1)}, bf16[4,272,512]{2,1,0:T(8,128)(2,1)}, u32[]{:S(2)}, u32[]{:S(2)}) collective-permute-start(bf16[4,272,512]{2,1,0:T(8,128)(2,1)} %get-tuple-element.225.part_b), channel_id=1, source_target_pairs={{0,16},{8,24},{16,0},{24,8},{1,17},{9,25},{17,1},{25,9},{2,18},{10... | collective-permute-start | bytes 3342344 | tf_op jit(solution)/shard_map/ppermute | solution.py:68
  133.6 40.7 %collective-permute-start.2 = (bf16[256,1024]{1,0:T(8,128)(2,1)}, bf16[256,1024]{1,0:T(8,128)(2,1)S(1)}, u32[]{:S(2)}, u32[]{:S(2)}) collective-permute-start(bf16[256,1024]{1,0:T(8,128)(2,1)} %collective-permute-done), channel_id=1, source_target_pairs={{0,16},{8,24},{16,0},{24,8},{1,17},{9,25},{17,1},{25,9},{2,18},{10... | collective-permute-start | bytes 1572872 | tf_op jit(solution)/shard_map/ppermute | solution.py:68
  164.3 84.8 %collective-permute-start.22 = (bf16[4,272,512]{2,1,0:T(8,128)(2,1)}, bf16[4,272,512]{2,1,0:T(8,128)(2,1)}, u32[]{:S(2)}, u32[]{:S(2)}) collective-permute-start(bf16[4,272,512]{2,1,0:T(8,128)(2,1)} %get-tuple-element.226.part_a), channel_id=1, source_target_pairs={{0,16},{8,24},{16,0},{24,8},{1,17},{9,25},{17,1},{25,9},{2,18},{10... | collective-permute-start | bytes 3342344 | tf_op jit(solution)/shard_map/ppermute | solution.py:68
  174.3 76.9 %collective-permute-start.18 = (bf16[4,272,512]{2,1,0:T(8,128)(2,1)}, bf16[4,272,512]{2,1,0:T(8,128)(2,1)S(1)}, u32[]{:S(2)}, u32[]{:S(2)}) collective-permute-start(bf16[4,272,512]{2,1,0:T(8,128)(2,1)} %get-tuple-element.226.part_a), channel_id=1, source_target_pairs={{0,8},{8,0},{16,24},{24,16},{1,9},{9,1},{17,25},{25,17},{2,10},{10... | collective-permute-start | bytes 3342344 | tf_op jit(solution)/shard_map/ppermute | solution.py:68
  241.9 49.6 %collective-permute-start.12 = (bf16[4,272,512]{2,1,0:T(8,128)(2,1)}, bf16[4,272,512]{2,1,0:T(8,128)(2,1)}, u32[]{:S(2)}, u32[]{:S(2)}) collective-permute-start(bf16[4,272,512]{2,1,0:T(8,128)(2,1)} %bitcast.18.part_a), channel_id=1, source_target_pairs={{0,8},{8,0},{16,24},{24,16},{1,9},{9,1},{17,25},{25,17},{2,10},{10... | collective-permute-start | bytes 3342344 | tf_op jit(solution)/shard_map/ppermute | solution.py:68
  249.1 72.1 %collective-permute-start.17 = (bf16[4,272,640]{2,1,0:T(8,128)(2,1)}, bf16[4,272,640]{2,1,0:T(8,128)(2,1)S(1)}, u32[]{:S(2)}, u32[]{:S(2)}) collective-permute-start(bf16[4,272,640]{2,1,0:T(8,128)(2,1)} %bitcast.19.part_b), channel_id=1, source_target_pairs={{0,8},{8,0},{16,24},{24,16},{1,9},{9,1},{17,25},{25,17},{2,10},{10... | collective-permute-start | bytes 4177928 | tf_op jit(solution)/shard_map/ppermute | solution.py:68
  251.2 61.5 %collective-permute-start.19 = (bf16[4,272,512]{2,1,0:T(8,128)(2,1)S(1)}, bf16[4,272,512]{2,1,0:T(8,128)(2,1)S(1)}, u32[]{:S(2)}, u32[]{:S(2)}) collective-permute-start(bf16[4,272,512]{2,1,0:T(8,128)(2,1)S(1)} %collective-permute-done.18.part_a), channel_id=1, source_target_pairs={{0,16},{8,24},{16,0},{24,8},{1,17},{9,25},{17,1},{25,9},{2,18},{10... | collective-permute-start | bytes 3342344 | tf_op jit(solution)/shard_map/ppermute | solution.py:68
  260.3 78.5 %collective-permute-start.15 = (bf16[4,272,640]{2,1,0:T(8,128)(2,1)}, bf16[4,272,640]{2,1,0:T(8,128)(2,1)S(1)}, u32[]{:S(2)}, u32[]{:S(2)}) collective-permute-start(bf16[4,272,640]{2,1,0:T(8,128)(2,1)} %collective-permute-done.14.part_b), channel_id=1, source_target_pairs={{0,8},{8,0},{16,24},{24,16},{1,9},{9,1},{17,25},{25,17},{2,10},{10... | collective-permute-start | bytes 4177928 | tf_op jit(solution)/shard_map/ppermute | solution.py:68
  267.5 63.0 %collective-permute-start.16 = (bf16[4,272,512]{2,1,0:T(8,128)(2,1)}, bf16[4,272,512]{2,1,0:T(8,128)(2,1)}, u32[]{:S(2)}, u32[]{:S(2)}) collective-permute-start(bf16[4,272,512]{2,1,0:T(8,128)(2,1)} %bitcast.18.part_a), channel_id=1, source_target_pairs={{0,16},{8,24},{16,0},{24,8},{1,17},{9,25},{17,1},{25,9},{2,18},{10... | collective-permute-start | bytes 3342344 | tf_op jit(solution)/shard_map/ppermute | solution.py:68
  291.4 47.4 %collective-permute-start.13 = (bf16[4,272,512]{2,1,0:T(8,128)(2,1)}, bf16[4,272,512]{2,1,0:T(8,128)(2,1)}, u32[]{:S(2)}, u32[]{:S(2)}) collective-permute-start(bf16[4,272,512]{2,1,0:T(8,128)(2,1)} %collective-permute-done.12.part_a), channel_id=1, source_target_pairs={{0,16},{8,24},{16,0},{24,8},{1,17},{9,25},{17,1},{25,9},{2,18},{10... | collective-permute-start | bytes 3342344 | tf_op jit(solution)/shard_map/ppermute | solution.py:68
  546.5 58.0 %collective-permute-start.33 = (bf16[4,272,640]{2,1,0:T(8,128)(2,1)}, bf16[4,272,640]{2,1,0:T(8,128)(2,1)S(1)}, u32[]{:S(2)}, u32[]{:S(2)}) collective-permute-start(bf16[4,272,640]{2,1,0:T(8,128)(2,1)} %get-tuple-element.121), channel_id=1, source_target_pairs={{0,16},{8,24},{16,0},{24,8},{1,17},{9,25},{17,1},{25,9},{2,18},{10... | collective-permute-start | bytes 4177928 | tf_op jit(solution)/shard_map/ppermute | solution.py:68
  724.2 605.6 %all-reduce.4.cloned.1.call-start = ((), (), s32[]{:S(2)}) async-start(), calls=%async_computation.5 | async-start | bytes 53608448 | tf_op jit(solution)/shard_map/psum | solution.py:854
  800.3 49.3 %collective-permute-start.27 = (bf16[4,272,512]{2,1,0:T(8,128)(2,1)}, bf16[4,272,512]{2,1,0:T(8,128)(2,1)S(1)}, u32[]{:S(2)}, u32[]{:S(2)}) collective-permute-start(bf16[4,272,512]{2,1,0:T(8,128)(2,1)} %get-tuple-element.113), channel_id=1, source_target_pairs={{0,16},{8,24},{16,0},{24,8},{1,17},{9,25},{17,1},{25,9},{2,18},{10... | collective-permute-start | bytes 3342344 | tf_op jit(solution)/shard_map/ppermute | solution.py:68
  827.5 46.9 %collective-permute-start.24 = (bf16[4,272,512]{2,1,0:T(8,128)(2,1)}, bf16[4,272,512]{2,1,0:T(8,128)(2,1)S(1)}, u32[]{:S(2)}, u32[]{:S(2)}) collective-permute-start(bf16[4,272,512]{2,1,0:T(8,128)(2,1)} %get-tuple-element.109), channel_id=1, source_target_pairs={{0,8},{8,0},{16,24},{24,16},{1,9},{9,1},{17,25},{25,17},{2,10},{10... | collective-permute-start | bytes 3342344 | tf_op jit(solution)/shard_map/ppermute | solution.py:68
  828.5 45.9 %collective-permute-start.26 = (bf16[4,272,512]{2,1,0:T(8,128)(2,1)S(1)}, bf16[4,272,512]{2,1,0:T(8,128)(2,1)S(1)}, u32[]{:S(2)}, u32[]{:S(2)}) collective-permute-start(bf16[4,272,512]{2,1,0:T(8,128)(2,1)S(1)} %add_convert_fusion.11), channel_id=1, source_target_pairs={{0,16},{8,24},{16,0},{24,8},{1,17},{9,25},{17,1},{25,9},{2,18},{10... | collective-permute-start | bytes 3342344 | tf_op jit(solution)/shard_map/ppermute | solution.py:68
  902.5 63.3 %all-to-all-start.2 = ((bf16[4,272,1024]{2,1,0:T(8,128)(2,1)}), bf16[4,272,1024]{2,1,0:T(8,128)(2,1)}, u32[]{:S(2)}, u32[]{:S(2)}) async-start(bf16[4,272,1024]{2,1,0:T(8,128)(2,1)} %bitcast.76), calls=%async_computation.2 | async-start | bytes 4456448 | tf_op jit(solution)/shard_map/all_to_all | solution.py:707
  (79 other events, 1174.5 us)
Sparse Core Ops, SparseCore 0:
  724.3 72.6 reduce-scatter.1
  800.8 528.9 all-reduce.3
